TPU v7x, 256 devices: a whole 4x4x8 slice. The times are simulated.
256 devices in a mesh: ctx: 32 (over y, x, core), head: 8 (over z).
Axes of the slice: x: 4, y: 4, z: 8, core: 2. Of those that a mesh axis runs over, the one named last changes fastest.
Arguments:
- x_in: bfloat16 [24576, 8192], P('ctx', 'head'), may hold values from -6 to 6
- z_in: bfloat16 [24576, 8192], P('ctx', 'head'), may hold values from -6 to 6
- bc_in: bfloat16 [24576, 2048], P('ctx', 'head'), may hold values from -6 to 6
- dt_in: bfloat16 [24576, 128], P('ctx', 'head'), may hold values from -4 to 4
- destination: int32 [24576], P('ctx'), may hold values from 0 to 24575, as said below
- doc_lengths: int32 [16], replicated, may hold values from 1 to 12288, 24576 in all
- conv_x: bfloat16 [4, 8192], P(None, 'head'), may hold values from -3 to 3
- conv_bc: bfloat16 [4, 2048], P(None, 'head'), may hold values from -3 to 3
- dt_bias: float32 [128], P('head'), may hold values from -4.5 to -3.5
- a_log: float32 [128], P('head'), may hold values from -12 to 1
- skip_gain: float32 [128], P('head'), may hold values from 0.5 to 1.5
- norm_gain: bfloat16 [8192], P('head'), may hold values from 0.25 to 1.75
- out_weight: bfloat16 [8192, 4096], P('head'), may hold values from -0.0625 to 0.0625
Outputs:
- mixed: bfloat16 [24576, 4096], P(('ctx', 'head'))
Inputs may be any that keep to these rules, and one draw needn't show every extreme that they name: destination is a permutation of the pack positions. Loader row i * 768 + j (shard i) goes to pack shard i, i + 1 or i - 1. Rows of shard i bound for shard i + 1 take the first positions of that shard, at most 384 of them; rows bound for shard i - 1 take its last positions, at most 384. Some loader shard sends exactly 384 rows to the next shard.
All inputs are finite; a program needn't handle non-finite values.
Results may differ from a plain program's by a relative error of at most 0.02.
Values may be sent and summed in bfloat16 or wider, within the bound.
A program may use at most 128 MiB of HBM per device.

v0:
```python
import jax
import jax.numpy as jnp
from jax import lax
from jax.sharding import PartitionSpec as P

N = 128
KCONV = 4
SPAN = 128


def padded(cells, sides, width):
    for axis, dim in sides:
        count = lax.axis_size(axis)
        ends = count - 1
        head = lax.slice_in_dim(cells, 0, width, axis=dim)
        tail = lax.slice_in_dim(cells, cells.shape[dim] - width, cells.shape[dim], axis=dim)
        cells = jnp.concatenate(
            [
                lax.ppermute(tail, axis, [(i, (i + 1) % count) for i in range(ends)]),
                cells,
                lax.ppermute(head, axis, [((i + 1) % count, i) for i in range(ends)]),
            ],
            axis=dim,
        )
    return cells


def passed_along(block, axis, distance):
    devices = range(lax.axis_size(axis))
    route = [(i - distance, i) for i in devices if i - distance in devices]
    return lax.ppermute(block, axis, route)


def prefix(x, axis, join, neutral):
    place = lax.axis_index(axis)
    gathered = jax.tree.map(
        lambda a, kind: lax.all_gather(a.astype(kind), axis), x, (jnp.bfloat16, jnp.bfloat16)
    )
    state = jax.tree.map(lambda a, e: jnp.zeros_like(a) + jnp.asarray(e, a.dtype), x, neutral)

    def one(lap, state):
        return join(
            state,
            jax.tree.map(
                lambda a, own: lax.dynamic_index_in_dim(a, lap, 0, False).astype(own.dtype),
                gathered,
                x,
            ),
        )

    return lax.fori_loop(0, place, one, state)


def doc_ids(doc_lengths, positions):
    doc_ends = jnp.cumsum(doc_lengths, dtype=jnp.int32)
    starts = doc_ends - doc_lengths
    counted = jnp.sum(
        (starts[None, :] <= positions[:, None]).astype(jnp.int32), axis=1, dtype=jnp.int32
    )
    return counted - 1


def ssd_block(
    carry_state, prev_doc, x_block, b_block, c_block, dt_block, rate_block, block_doc, skip_gain
):
    block_len = block_doc.shape[0]
    cum_rate = jnp.cumsum(rate_block, axis=0)
    ordinal = jnp.arange(block_len, dtype=jnp.int32)
    same_doc = (block_doc[:, None] == block_doc[None, :]) & (ordinal[None, :] <= ordinal[:, None])
    cum_t = jnp.moveaxis(cum_rate, 0, -1)
    rate_gap = cum_t[..., :, None] - cum_t[..., None, :]
    decay_mat = jnp.where(same_doc, jnp.exp(jnp.where(same_doc, rate_gap, 0.0)), 0.0)
    scores = jnp.einsum("tgn,sgn->gts", c_block, b_block, preferred_element_type=jnp.float32)
    dt_t = jnp.moveaxis(dt_block, 0, -1)
    mixing = (decay_mat * scores[:, None] * dt_t[:, :, None, :]).astype(jnp.bfloat16)
    inner_part = jnp.einsum("ghts,sghp->tghp", mixing, x_block, preferred_element_type=jnp.float32)
    linked = (block_doc == prev_doc).astype(jnp.float32)
    entry_fac = jnp.exp(cum_rate) * linked[:, None, None]
    from_state = (
        jnp.einsum(
            "tgn,ghpn->tghp",
            c_block,
            carry_state.astype(jnp.bfloat16),
            preferred_element_type=jnp.float32,
        )
        * entry_fac[..., None]
    )
    y_block = inner_part + from_state + skip_gain[None, :, :, None] * x_block.astype(jnp.float32)
    tail_doc = (block_doc == block_doc[-1]).astype(jnp.float32)
    weight = jnp.exp(cum_rate[-1][None] - cum_rate) * tail_doc[:, None, None] * dt_block
    weighted_x = (weight[..., None] * x_block.astype(jnp.float32)).astype(jnp.bfloat16)
    carried = jnp.exp(cum_rate[-1]) * (block_doc[-1] == prev_doc).astype(jnp.float32)
    new_state = carry_state * carried[..., None, None] + jnp.einsum(
        "sghp,sgn->ghpn", weighted_x, b_block, preferred_element_type=jnp.float32
    )
    return (new_state, y_block)


def gated_norm(y_rows, z_rows, norm_gain, groups):
    gated = y_rows.astype(jnp.float32) * jax.nn.silu(z_rows.astype(jnp.float32))
    row_count = gated.shape[0]
    grouped = gated.reshape(row_count, groups, -1)
    inv_rms = lax.rsqrt(jnp.mean(grouped * grouped, axis=-1, keepdims=True) + 1e-05)
    return ((grouped * inv_rms).reshape(row_count, -1) * norm_gain.astype(jnp.float32)).astype(
        jnp.bfloat16
    )


def to_loader(block, destination, first_pos, margin):
    framed = padded(block, (("ctx", 0),), margin)
    return framed[destination - first_pos + margin]


def per_device(
    x_in,
    z_in,
    bc_in,
    dt_in,
    destination,
    doc_lengths,
    conv_x,
    conv_bc,
    dt_bias,
    a_log,
    skip_gain,
    norm_gain,
    out_weight,
):
    tok_rows = x_in.shape[0]
    channels = x_in.shape[1]
    heads_here = dt_in.shape[1]
    head_size = channels // heads_here
    bc_width = bc_in.shape[1]
    state_size = conv_bc.shape[1] * 0 + N
    groups_here = bc_width // (2 * state_size)
    per_group = heads_here // groups_here
    margin = tok_rows // 2
    shard_id = lax.axis_index("ctx")
    first_pos = shard_id * tok_rows
    target = destination // tok_rows
    offset = destination - target * tok_rows
    relative = target - shard_id
    payload = jnp.concatenate([x_in, bc_in, dt_in], axis=1)
    col_count = payload.shape[1]
    slot_index = jnp.where(
        relative == -1,
        offset - (tok_rows - margin),
        jnp.where(relative == 1, margin + offset, 2 * margin),
    )
    outgoing = (
        jnp.zeros((2 * margin + 1, col_count), jnp.bfloat16)
        .at[slot_index]
        .set(payload)[: 2 * margin]
    )
    home_slot = jnp.where(relative == 0, offset, tok_rows)
    packed = (
        jnp.zeros((tok_rows + 1, col_count), jnp.bfloat16).at[home_slot].set(payload)[:tok_rows]
    )
    framed = padded(outgoing, (("ctx", 0),), margin)
    packed = (
        packed.at[:margin].add(framed[:margin]).at[tok_rows - margin :].add(framed[3 * margin :])
    )
    xbc_width = channels + bc_width
    rim_rows = passed_along(packed[tok_rows - (KCONV - 1) :, :xbc_width], "ctx", 1)
    extended = jnp.concatenate([rim_rows, packed[:, :xbc_width]], axis=0)
    ext_pos = first_pos - (KCONV - 1) + jnp.arange(tok_rows + KCONV - 1, dtype=jnp.int32)
    ext_doc = doc_ids(doc_lengths, ext_pos)
    doc_here = ext_doc[KCONV - 1 :]
    doc_before = ext_doc[KCONV - 2]
    kernel = jnp.concatenate([conv_x, conv_bc], axis=1).astype(jnp.float32)
    conv_sum = jnp.zeros((tok_rows, xbc_width), jnp.float32)
    for tap in range(KCONV):
        usable = (ext_doc[tap : tap + tok_rows] == doc_here).astype(jnp.float32)
        conv_sum = (
            conv_sum
            + kernel[tap] * extended[tap : tap + tok_rows].astype(jnp.float32) * usable[:, None]
        )
    conv_out = jax.nn.silu(conv_sum).astype(jnp.bfloat16)
    x_heads = conv_out[:, :channels].reshape(tok_rows, groups_here, per_group, head_size)
    bc_heads = conv_out[:, channels:].reshape(tok_rows, groups_here, 2, state_size)
    c_heads = bc_heads[:, :, 1]
    dt_step = jax.nn.softplus(
        packed[:, xbc_width : xbc_width + heads_here].astype(jnp.float32) + dt_bias
    )
    log_decay = (dt_step * -jnp.exp(a_log)).reshape(tok_rows, groups_here, per_group)
    dt_grid = dt_step.reshape(tok_rows, groups_here, per_group)
    skip_grid = skip_gain.reshape(groups_here, per_group)
    num_blocks = tok_rows // SPAN
    sequence = (
        x_heads.reshape(num_blocks, SPAN, groups_here, per_group, head_size),
        bc_heads[:, :, 0].reshape(num_blocks, SPAN, groups_here, state_size),
        c_heads.reshape(num_blocks, SPAN, groups_here, state_size),
        dt_grid.reshape(num_blocks, SPAN, groups_here, per_group),
        log_decay.reshape(num_blocks, SPAN, groups_here, per_group),
        doc_here.reshape(num_blocks, SPAN),
    )

    def advance(state_pair, entry_item):
        carry_state, prev_doc = state_pair
        x_block, b_block, c_block, dt_block, rate_block, block_doc = entry_item
        new_state, y_block = ssd_block(
            carry_state,
            prev_doc,
            x_block,
            b_block,
            c_block,
            dt_block,
            rate_block,
            block_doc,
            skip_grid,
        )
        return ((new_state, block_doc[-1]), y_block)

    empty_state = jnp.zeros((groups_here, per_group, head_size, state_size), jnp.float32)
    (local_state, _), y_blocks = lax.scan(advance, (empty_state, doc_before), sequence)
    shard_rate = jnp.cumsum(log_decay, axis=0)
    linked = (doc_here == doc_before).astype(jnp.float32)
    entry_decay = jnp.exp(shard_rate) * linked[:, None, None]
    shard_decay = entry_decay[-1]

    def compose(earlier, later):
        return (earlier[0] * later[0], later[0][..., None, None] * earlier[1] + later[1])

    incoming = prefix(
        (shard_decay, local_state),
        "ctx",
        compose,
        (jnp.ones_like(shard_decay), jnp.zeros_like(local_state)),
    )[1]
    correction = (
        jnp.einsum(
            "tgn,ghpn->tghp",
            c_heads,
            incoming.astype(jnp.bfloat16),
            preferred_element_type=jnp.float32,
        )
        * entry_decay[..., None]
    )
    y_local = y_blocks.reshape(tok_rows, groups_here, per_group, head_size)
    y_pack = (y_local + correction).reshape(tok_rows, channels).astype(jnp.bfloat16)
    y_loader = to_loader(y_pack, destination, first_pos, margin)
    normed = gated_norm(y_loader, z_in, norm_gain, groups_here)
    mixed = lax.psum_scatter(
        jnp.dot(normed, out_weight, preferred_element_type=jnp.float32).astype(jnp.bfloat16),
        "head",
        scatter_dimension=0,
        tiled=True,
    )
    return mixed


def solution(mesh):
    placed = (
        P("ctx", "head"),
        P("ctx", "head"),
        P("ctx", "head"),
        P("ctx", "head"),
        P("ctx"),
        P(),
        P(None, "head"),
        P(None, "head"),
        P("head"),
        P("head"),
        P("head"),
        P("head"),
        P("head", None),
    )
    return jax.shard_map(
        per_device, mesh=mesh, in_specs=placed, out_specs=P(("ctx", "head"), None), check_vma=False
    )
```

profile of v0, /device:TPU:24, one launch (start us, length us, event | category | flops | bytes accessed | tf_op | source)
XLA Modules:
  0.0 426.8 jit_solution(14231732986993484993)
XLA Ops:
  7.4 1.3 compare_select_fusion.1
  8.7 8.0 %scatter_custom_fusion.1 = bf16[769,1296]{1,0:T(8,128)(2,1)S(1)} fusion(s32[768]{0:T(1024)S(1)} %get-tuple-element.334, bf16[]{:T(256)} %constant.145.clone.1, bf16[768,16]{1,0:T(8,128)(2,1)S(1)} %copy.168, bf16[]{:T(256)} %constant.160, bf16[768,256]{1,0:T(8,128)(2,1)} %param.23, bf16[768,1024]{1,0:T(8,128)(2,1)} %param.21), kind=kCustom, calls=%fused_computation.86 | custom fusion | flops 5971968 | bytes 4155940 | tf_op jit(solution)/shard_map/scatter | solution.py:153
  17.9 2.3 copy.171
  20.2 1.9 collective-permute-start
  22.2 1.4 copy.172
  23.6 5.7 %collective-permute-start.1 = (bf16[384,1296]{0,1:T(8,128)(2,1)}, bf16[384,1296]{0,1:T(8,128)(2,1)}, u32[]{:S(2)}, u32[]{:S(2)}) collective-permute-start(bf16[384,1296]{0,1:T(8,128)(2,1)} %copy.172), channel_id=1, source_target_pairs={{8,0},{16,8},{24,16},{32,24},{40,32},{48,40},{56,48},{64,56},{72,6... | collective-permute-start | bytes 2985992 | tf_op jit(solution)/shard_map/ppermute | solution.py:21
  29.3 8.0 %scatter_custom_fusion = bf16[769,1296]{1,0:T(8,128)(2,1)S(1)} fusion(s32[768]{0:T(1024)S(1)} %get-tuple-element.335, bf16[]{:T(256)} %constant.145.clone.1, bf16[768,16]{1,0:T(8,128)(2,1)S(1)} %copy.168, bf16[]{:T(256)} %constant.160, bf16[768,256]{1,0:T(8,128)(2,1)} %param.23, bf16[768,1024]{1,0:T(8,128)(2,1)} %param.21), kind=kCustom, calls=%fused_computation.88 | custom fusion | flops 5971968 | bytes 4155940 | tf_op jit(solution)/shard_map/scatter | solution.py:157
  38.5 1.5 slice.178
  40.9 2.0 copy.195
  43.0 2.7 copy.194
  48.3 1.6 add_dynamic-update-slice_fusion
  49.9 1.7 constant_dynamic-update-slice_fusion
  51.7 2.1 collective-permute-start.2
  54.0 1.4 slice.186
  56.3 6.1 %collective-permute-done.2 = bf16[3,1280]{0,1:T(8,128)(2,1)S(1)} collective-permute-done((bf16[3,1280]{0,1:T(8,128)(2,1)S(1)}, bf16[3,1280]{0,1:T(8,128)(2,1)S(1)}, u32[]{:S(2)}, u32[]{:S(2)}) %collective-permute-start.2) | collective-permute-done | bytes 7712 | tf_op jit(solution)/shard_map/ppermute | solution.py:31
  62.4 8.6 %multiply_convert_fusion.2 = bf16[768,1280]{0,1:T(8,128)(2,1)S(1)} fusion(bf16[768,1280]{0,1:T(8,128)(2,1)} %slice.186, bf16[3,1280]{0,1:T(8,128)(2,1)S(1)} %collective-permute-done.2, f32[1280]{0:T(1024)S(1)} %get-tuple-element.283, f32[768]{0:T(1024)S(1)} %get-tuple-element.337, f32[1280]{0:T(1024)S(1)} %get-tuple-element.284, f32[768]{0:T(1024)S(1)} %copy-done.4, ...), kind=kLoop, calls=%fused_computation.65 | loop fusion | flops 27525120 | bytes 3969536 | tf_op jit(solution)/shard_map/convert_element_type | solution.py:178
  72.7 3.4 reshape_reshape.11
  76.1 1.6 copy.177
  77.7 130.2 %while.30 = (s32[]{:T(128)}, f32[1,16,64,128]{3,2,1,0:T(8,128)S(1)}, s32[]{:T(128)}, f32[6,128,1,16,64]{1,0,4,3,2:T(8,128)}, f32[6,128,1,16]{3,1,2,0:T(8,128)}, ...) while((s32[]{:T(128)}, ...), condition=%wide.region_6.7_spmd.clone, body=%wide.region_4.6_spmd.clone.sunk | while | flops 108321296 | bytes 5440525 | solution.py:215
  82.3 1.6 fusion.110
  85.1 14.2 %dynamic_update_slice.6 = f32[6,128,1,16,64]{1,0,4,3,2:T(8,128)} dynamic-update-slice(f32[6,128,1,16,64]{1,0,4,3,2:T(8,128)} %get-tuple-element.463, f32[1,128,1,16,64]{1,0,4,3,2:T(1,128)S(1)} %bitcast.221, s32[]{:T(128)S(6)} %copy.220, s32[]{:T(128)} %constant.138.clone.1..sunk.1, s32[]{:T(128)} %constant.138.clone.1..sunk.1, s32[]{:T(128)} %constant.138.clone.1..sunk.1, s32[]{:T(128)} %constant.138.clone.1..sunk.1) | dynamic-update-slice | bytes 1048580 | tf_op jit(solution)/shard_map/while/body/jit(dynamic_update_index_in_dim)/dynamic_update_slice | solution.py:215
  104.0 1.6 fusion.110
  106.8 14.2 %dynamic_update_slice.6 = f32[6,128,1,16,64]{1,0,4,3,2:T(8,128)} dynamic-update-slice(f32[6,128,1,16,64]{1,0,4,3,2:T(8,128)} %get-tuple-element.463, f32[1,128,1,16,64]{1,0,4,3,2:T(1,128)S(1)} %bitcast.221, s32[]{:T(128)S(6)} %copy.220, s32[]{:T(128)} %constant.138.clone.1..sunk.1, s32[]{:T(128)} %constant.138.clone.1..sunk.1, s32[]{:T(128)} %constant.138.clone.1..sunk.1, s32[]{:T(128)} %constant.138.clone.1..sunk.1) | dynamic-update-slice | bytes 1048580 | tf_op jit(solution)/shard_map/while/body/jit(dynamic_update_index_in_dim)/dynamic_update_slice | solution.py:215
  125.7 1.6 fusion.110
  128.5 14.2 %dynamic_update_slice.6 = f32[6,128,1,16,64]{1,0,4,3,2:T(8,128)} dynamic-update-slice(f32[6,128,1,16,64]{1,0,4,3,2:T(8,128)} %get-tuple-element.463, f32[1,128,1,16,64]{1,0,4,3,2:T(1,128)S(1)} %bitcast.221, s32[]{:T(128)S(6)} %copy.220, s32[]{:T(128)} %constant.138.clone.1..sunk.1, s32[]{:T(128)} %constant.138.clone.1..sunk.1, s32[]{:T(128)} %constant.138.clone.1..sunk.1, s32[]{:T(128)} %constant.138.clone.1..sunk.1) | dynamic-update-slice | bytes 1048580 | tf_op jit(solution)/shard_map/while/body/jit(dynamic_update_index_in_dim)/dynamic_update_slice | solution.py:215
  147.4 1.6 fusion.110
  150.2 14.2 %dynamic_update_slice.6 = f32[6,128,1,16,64]{1,0,4,3,2:T(8,128)} dynamic-update-slice(f32[6,128,1,16,64]{1,0,4,3,2:T(8,128)} %get-tuple-element.463, f32[1,128,1,16,64]{1,0,4,3,2:T(1,128)S(1)} %bitcast.221, s32[]{:T(128)S(6)} %copy.220, s32[]{:T(128)} %constant.138.clone.1..sunk.1, s32[]{:T(128)} %constant.138.clone.1..sunk.1, s32[]{:T(128)} %constant.138.clone.1..sunk.1, s32[]{:T(128)} %constant.138.clone.1..sunk.1) | dynamic-update-slice | bytes 1048580 | tf_op jit(solution)/shard_map/while/body/jit(dynamic_update_index_in_dim)/dynamic_update_slice | solution.py:215
  169.1 1.6 fusion.110
  171.9 14.2 %dynamic_update_slice.6 = f32[6,128,1,16,64]{1,0,4,3,2:T(8,128)} dynamic-update-slice(f32[6,128,1,16,64]{1,0,4,3,2:T(8,128)} %get-tuple-element.463, f32[1,128,1,16,64]{1,0,4,3,2:T(1,128)S(1)} %bitcast.221, s32[]{:T(128)S(6)} %copy.220, s32[]{:T(128)} %constant.138.clone.1..sunk.1, s32[]{:T(128)} %constant.138.clone.1..sunk.1, s32[]{:T(128)} %constant.138.clone.1..sunk.1, s32[]{:T(128)} %constant.138.clone.1..sunk.1) | dynamic-update-slice | bytes 1048580 | tf_op jit(solution)/shard_map/while/body/jit(dynamic_update_index_in_dim)/dynamic_update_slice | solution.py:215
  190.8 1.6 fusion.110
  193.6 14.2 %dynamic_update_slice.6 = f32[6,128,1,16,64]{1,0,4,3,2:T(8,128)} dynamic-update-slice(f32[6,128,1,16,64]{1,0,4,3,2:T(8,128)} %get-tuple-element.463, f32[1,128,1,16,64]{1,0,4,3,2:T(1,128)S(1)} %bitcast.221, s32[]{:T(128)S(6)} %copy.220, s32[]{:T(128)} %constant.138.clone.1..sunk.1, s32[]{:T(128)} %constant.138.clone.1..sunk.1, s32[]{:T(128)} %constant.138.clone.1..sunk.1, s32[]{:T(128)} %constant.138.clone.1..sunk.1) | dynamic-update-slice | bytes 1048580 | tf_op jit(solution)/shard_map/while/body/jit(dynamic_update_index_in_dim)/dynamic_update_slice | solution.py:215
  208.7 1.7 reduce-window.20
  211.0 18.8 %all_gather.10 = bf16[32,1,16]{2,1,0:T(2,128)(2,1)S(1)} all-gather(bf16[1,1,16]{2,1,0:T(2,128)(2,1)S(1)} %copy.184), channel_id=1, replica_groups=mesh['ctx'=32,'head'=8] {'ctx'}, dimensions={0}, use_global_device_ids=true | all-gather | bytes 1056 | tf_op jit(solution)/shard_map/all_gather | solution.py:37
  229.9 4.8 %reshape.383 = f32[768,1,16,64]{0,3,2,1:T(8,128)} reshape(f32[6,128,1,16,64]{1,0,4,3,2:T(8,128)} %get-tuple-element.131) | data formatting | bytes 6291456 | tf_op jit(solution)/shard_map/reshape | solution.py:239
  234.7 32.0 %all-gather.3.cloned.1.call-done = bf16[32,16,64,128]{3,2,1,0:T(8,128)(2,1)} async-done(((bf16[1,16,64,128]{3,2,1,0:T(8,128)(2,1)}), bf16[32,16,64,128]{3,2,1,0:T(8,128)(2,1)}) %all-gather.3.cloned.1.call-update) | async-done | bytes 8388624 | tf_op jit(solution)/shard_map/all_gather | solution.py:37
  266.7 27.6 %while.29 = (s32[]{:T(128)}, f32[1,16,64,128]{3,2,1,0:T(8,128)S(1)}, s32[]{:T(128)}, bf16[32,1,16]{2,1,0:T(2,128)(2,1)S(1)}, bf16[32,1,16,64,128]{4,3,2,1,0:T(8,128)(2,1)}, /*index=5*/s32[]{:T(128)}, s32[]{:T(128)}, s32[]{:T(128)}) while((s32[]{:T(128)}, f32[1,16,64,128]{3,2,1,0:T(8,128)S(1)}, s32[]{:T(128)}, ...), condition=%wide.region_10.11_spmd, body=%wide.region_9.10_spmd.sunk | while | flops 393237 | bytes 1311015 | solution.py:51
  294.4 2.4 fusion.47
  298.0 2.3 copy.186
  301.5 2.1 collective-permute-start.4
  303.7 3.3 collective-permute-start.3
  307.0 1.7 copy.188
  308.7 4.8 %collective-permute-done.4 = bf16[384,1024]{1,0:T(8,128)(2,1)S(1)} collective-permute-done((bf16[384,1024]{1,0:T(8,128)(2,1)}, bf16[384,1024]{1,0:T(8,128)(2,1)S(1)}, u32[]{:S(2)}, u32[]{:S(2)}) %collective-permute-start.4) | collective-permute-done | bytes 786464 | tf_op jit(solution)/shard_map/ppermute | solution.py:21
  314.3 5.1 %collective-permute-done.3 = bf16[384,1024]{1,0:T(8,128)(2,1)} collective-permute-done((bf16[384,1024]{1,0:T(8,128)(2,1)}, bf16[384,1024]{1,0:T(8,128)(2,1)}, u32[]{:S(2)}, u32[]{:S(2)}) %collective-permute-start.3) | collective-permute-done | bytes 786464 | tf_op jit(solution)/shard_map/ppermute | solution.py:19
  319.4 2.1 pad_maximum_fusion
  321.5 3.6 gather_fusion
  325.1 3.1 multiply_reduce_fusion
  328.2 12.9 %convolution_convert_fusion = bf16[768,4096]{1,0:T(8,128)(2,1)} fusion(bf16[1024,4096]{1,0:T(8,128)(2,1)} %param.33, f32[1024]{0:T(1024)S(1)} %convert_element_type.171, f32[768]{0:T(1024)S(1)} %add_rsqrt_fusion, bf16[768,1024]{1,0:T(8,128)(2,1)S(1)} %copy-done.1, bf16[768,1024]{1,0:T(8,128)(2,1)S(1)} %copy-done), kind=kOutput, calls=%fused_computation.62 | convolution fusion | flops 6453460992 | bytes 17832960 | tf_op jit(solution)/shard_map/dot_general | solution.py:244
  341.2 78.8 %reduce-scatter.2.cloned.1.call-done = bf16[96,4096]{1,0:T(8,128)(2,1)} async-done(((bf16[768,4096]{1,0:T(8,128)(2,1)}), bf16[96,4096]{1,0:T(8,128)(2,1)}) %reduce-scatter.2.cloned.1.call-update) | async-done | bytes 786448 | tf_op jit(solution)/shard_map/reduce_scatter | solution.py:243
  (218 shorter events, 69.1 us)
Async XLA Ops:
  6.5 260.2 %all-gather.3.cloned.1.call-start = ((), (), s32[]{:S(2)}) async-start(), calls=%async_computation.2 | async-start | bytes 8650752 | tf_op jit(solution)/shard_map/all_gather | solution.py:37
  20.2 28.0 %collective-permute-start = (bf16[384,1296]{0,1:T(8,128)(2,1)}, bf16[384,1296]{0,1:T(8,128)(2,1)}, u32[]{:S(2)}, u32[]{:S(2)}) collective-permute-start(bf16[384,1296]{0,1:T(8,128)(2,1)} %copy.171), channel_id=1, source_target_pairs={{0,8},{8,16},{16,24},{24,32},{32,40},{40,48},{48,56},{56,64},{64,7... | collective-permute-start | bytes 2985992 | tf_op jit(solution)/shard_map/ppermute | solution.py:19
  23.6 26.3 %collective-permute-start.1 = (bf16[384,1296]{0,1:T(8,128)(2,1)}, bf16[384,1296]{0,1:T(8,128)(2,1)}, u32[]{:S(2)}, u32[]{:S(2)}) collective-permute-start(bf16[384,1296]{0,1:T(8,128)(2,1)} %copy.172), channel_id=1, source_target_pairs={{8,0},{16,8},{24,16},{32,24},{40,32},{48,40},{56,48},{64,56},{72,6... | collective-permute-start | bytes 2985992 | tf_op jit(solution)/shard_map/ppermute | solution.py:21
  37.4 2.6 copy-start.11
  40.0 5.7 %copy-start.7 = (bf16[4,1024]{1,0:T(4,128)(2,1)S(1)}, bf16[4,1024]{1,0:T(4,128)(2,1)}, u32[]{:S(2)}) copy-start(bf16[4,1024]{1,0:T(4,128)(2,1)} %param.27) | copy-start | bytes 24580
  40.0 5.7 %copy-start.9 = (bf16[4,256]{1,0:T(4,128)(2,1)S(1)}, bf16[4,256]{1,0:T(4,128)(2,1)}, u32[]{:S(2)}) copy-start(bf16[4,256]{1,0:T(4,128)(2,1)} %param.28) | copy-start | bytes 6148
  40.9 6.1 %copy-start.12 = (f32[16]{0:T(128)S(1)}, f32[16]{0:T(128)}, u32[]{:S(2)}) copy-start(f32[16]{0:T(128)} %param.30) | copy-start | bytes 196
  48.3 5.6 %copy-start.10 = (f32[16]{0:T(128)S(1)}, f32[16]{0:T(128)}, u32[]{:S(2)}) copy-start(f32[16]{0:T(128)} %param.29) | copy-start | bytes 196
  51.6 10.9 %copy-start.3 = (f32[1280]{0:T(1024)S(1)}, f32[1280]{0:T(1024)}, u32[]{:S(2)}) copy-start(f32[1280]{0:T(1024)} %get-tuple-element.285) | copy-start | bytes 15364
  51.6 10.9 %copy-start.4 = (f32[768]{0:T(1024)S(1)}, f32[768]{0:T(1024)}, u32[]{:S(2)}) copy-start(f32[768]{0:T(1024)} %get-tuple-element.338) | copy-start | bytes 9220
  51.6 10.9 %copy-start.5 = (f32[768]{0:T(1024)S(1)}, f32[768]{0:T(1024)}, u32[]{:S(2)}) copy-start(f32[768]{0:T(1024)} %get-tuple-element.339) | copy-start | bytes 9220
  51.7 10.7 %collective-permute-start.2 = (bf16[3,1280]{0,1:T(8,128)(2,1)S(1)}, bf16[3,1280]{0,1:T(8,128)(2,1)S(1)}, u32[]{:S(2)}, u32[]{:S(2)}) collective-permute-start(bf16[3,1280]{0,1:T(8,128)(2,1)S(1)} %slice.185), channel_id=1, source_target_pairs={{0,8},{8,16},{16,24},{24,32},{32,40},{40,48},{48,56},{56,64},{64,7... | collective-permute-start | bytes 23048 | tf_op jit(solution)/shard_map/ppermute | solution.py:31
  72.7 5.0 %copy-start.13 = (f32[16]{0:T(128)S(1)}, f32[16]{0:T(128)}, u32[]{:S(2)}) copy-start(f32[16]{0:T(128)} %param.31) | copy-start | bytes 196
  208.6 211.4 %reduce-scatter.2.cloned.1.call-start = ((), (), s32[]{:S(2)}) async-start(), calls=%async_computation.1 | async-start | bytes 7077888 | tf_op jit(solution)/shard_map/reduce_scatter | solution.py:243
  296.8 10.1 %copy-start.8 = (bf16[1024]{0:T(1024)(128)(2,1)S(1)}, bf16[1024]{0:T(1024)(128)(2,1)}, u32[]{:S(2)}) copy-start(bf16[1024]{0:T(1024)(128)(2,1)} %param.32) | copy-start | bytes 6148
  296.9 10.1 %copy-start.6 = (s32[768]{0:T(1024)S(1)}, s32[768]{0:T(1024)}, u32[]{:S(2)}) copy-start(s32[768]{0:T(1024)} %get-tuple-element.333) | copy-start | bytes 9220
  301.5 12.0 %collective-permute-start.4 = (bf16[384,1024]{1,0:T(8,128)(2,1)}, bf16[384,1024]{1,0:T(8,128)(2,1)S(1)}, u32[]{:S(2)}, u32[]{:S(2)}) collective-permute-start(bf16[384,1024]{1,0:T(8,128)(2,1)} %copy.187), channel_id=1, source_target_pairs={{8,0},{16,8},{24,16},{32,24},{40,32},{48,40},{56,48},{64,56},{72,6... | collective-permute-start | bytes 2359304 | tf_op jit(solution)/shard_map/ppermute | solution.py:21
  303.7 15.7 %collective-permute-start.3 = (bf16[384,1024]{1,0:T(8,128)(2,1)}, bf16[384,1024]{1,0:T(8,128)(2,1)}, u32[]{:S(2)}, u32[]{:S(2)}) collective-permute-start(bf16[384,1024]{1,0:T(8,128)(2,1)} %copy.186), channel_id=1, source_target_pairs={{0,8},{8,16},{16,24},{24,32},{32,40},{40,48},{48,56},{56,64},{64,7... | collective-permute-start | bytes 2359304 | tf_op jit(solution)/shard_map/ppermute | solution.py:19
  313.5 0.9 copy-start.2
  325.1 3.1 copy-start
  325.1 3.1 copy-start.1
Sparse Core Ops, SparseCore 0:
  208.8 57.8 all-gather.2
  341.3 78.6 reduce-scatter.1
where the time goes:
time: 433 us; the launch traced here: 427 us
  local copies, waits for them, and re-layouts  135 us (31%)
  waiting for transfers between devices  127 us (29%)
  other arithmetic  74.7 us (17%)
  matrix products  34.7 us (8%)
  blocking collectives  18.8 us (4%)
  starting transfers between devices  15.2 us (4%)
  between operations  13.8 us (3%)
  loops' own time  7.76 us (2%)
    dynamic_update_slice x6, local copies, waits for them, and re-layouts, per_device(): lax.scan(advance, (empty_state, doc_before), sequence)  85.4 us
    reduce_scatter x1, waiting for transfers between devices, per_device(): lax.psum_scatter(jnp.dot(normed, out_weight, preferred_element_type=jnp.f...  78.8 us
    all_gather x1, waiting for transfers between devices, prefix(): lax.all_gather(a.astype(kind), axis)  32 us
    add x24, other arithmetic, compose(): later[0][..., None, None] * earlier[1] + later[1]  26.7 us
    all_gather x1, blocking collectives, prefix(): lax.all_gather(a.astype(kind), axis)  18.8 us
    dot_general x1, matrix products, per_device(): jnp.dot(normed, out_weight, preferred_element_type=jnp.float32)  12.9 us
    dot_general x6, matrix products, ssd_block(): jnp.einsum('ghts,sghp->tghp', mixing, x_block, preferred_element_type=jnp...  9.67 us
    unnamed x34, local copies, waits for them, and re-layouts  9.26 us
  transfers between devices with their start and end apart: 7, of which 5 were waited for; matrix products, arithmetic and copies ran while one was open for 8% of the time, Pallas kernels for 0%

commit v1 on v0

--- a/solution.py
+++ b/solution.py
@@ -1,6 +1,8 @@
 import jax
 import jax.numpy as jnp
 from jax import lax
+from jax.experimental import pallas as pl
+from jax.experimental.pallas import tpu as pltpu
 from jax.sharding import PartitionSpec as P
 
 N = 128
@@ -109,6 +111,105 @@
 def to_loader(block, destination, first_pos, margin):
     framed = padded(block, (("ctx", 0),), margin)
     return framed[destination - first_pos + margin]
+
+
+SUBS = 4
+
+
+def ring_kernel(normed_ref, w_hbm, out_ref, w_ref, sbuf, rbuf, w_sems, send_sems, recv_sems):
+    n = lax.axis_size("head")
+    me = lax.axis_index("head")
+    rows = out_ref.shape[0]
+    wide = w_ref.shape[1]
+    width = wide // (2 * SUBS)
+    barrier = pltpu.get_barrier_semaphore()
+    loads = []
+    for sub in range(SUBS):
+        for way in range(2):
+            cols = pl.ds((way * SUBS + sub) * width, width)
+            loads.append(
+                pltpu.make_async_copy(w_hbm.at[:, cols], w_ref.at[:, cols], w_sems.at[way, sub])
+            )
+    for load in loads:
+        load.start()
+    hops = (lax.rem(me + 1, n), lax.rem(me + n - 1, n))
+    for hop in hops:
+        pl.semaphore_signal(barrier, inc=1, device_id={"head": hop})
+    rbuf[0] = jnp.zeros_like(rbuf[0])
+    pl.semaphore_wait(barrier, 2)
+    for load in loads:
+        load.wait()
+
+    def copy(step, way, sub):
+        return pltpu.make_async_remote_copy(
+            src_ref=sbuf.at[step, way, sub],
+            dst_ref=rbuf.at[step + 1, way, sub],
+            send_sem=send_sems.at[step, way, sub],
+            recv_sem=recv_sems.at[step, way, sub],
+            device_id={"head": hops[way]},
+        )
+
+    def one(step, _):
+        for sub in range(SUBS):
+            for way in range(2):
+                chunk = lax.rem(me + 2 * n - 1 - step, n) if way == 0 else lax.rem(me + 1 + step, n)
+                begin = (way * SUBS + sub) * width
+                part = jnp.dot(
+                    normed_ref[pl.ds(pl.multiple_of(chunk * rows, rows), rows), :],
+                    w_ref[:, begin : begin + width],
+                    preferred_element_type=jnp.float32,
+                )
+
+                @pl.when(step > 0)
+                def _():
+                    copy(step - 1, way, sub).wait_recv()
+
+                total = (part + rbuf[step, way, sub].astype(jnp.float32)).astype(jnp.bfloat16)
+
+                @pl.when(step < n - 1)
+                def _():
+                    sbuf[step, way, sub] = total
+                    copy(step, way, sub).start()
+
+                @pl.when(step == n - 1)
+                def _():
+                    out_ref[:, begin : begin + width] = total
+
+        return 0
+
+    lax.fori_loop(0, n, one, 0)
+
+    def drain(step, _):
+        for sub in range(SUBS):
+            for way in range(2):
+                copy(step, way, sub).wait_send()
+        return 0
+
+    lax.fori_loop(0, n - 1, drain, 0)
+
+
+def project_scatter(normed, out_weight):
+    n = lax.axis_size("head")
+    rows = normed.shape[0] // n
+    depth, wide = out_weight.shape
+    width = wide // (2 * SUBS)
+    return pl.pallas_call(
+        ring_kernel,
+        out_shape=jax.ShapeDtypeStruct((rows, wide), jnp.bfloat16),
+        in_specs=[pl.BlockSpec(memory_space=pltpu.VMEM), pl.BlockSpec(memory_space=pl.ANY)],
+        out_specs=pl.BlockSpec(memory_space=pltpu.VMEM),
+        scratch_shapes=[
+            pltpu.VMEM((depth, wide), jnp.bfloat16),
+            pltpu.VMEM((n - 1, 2, SUBS, rows, width), jnp.bfloat16),
+            pltpu.VMEM((n, 2, SUBS, rows, width), jnp.bfloat16),
+            pltpu.SemaphoreType.DMA((2, SUBS)),
+            pltpu.SemaphoreType.DMA((n - 1, 2, SUBS)),
+            pltpu.SemaphoreType.DMA((n - 1, 2, SUBS)),
+        ],
+        compiler_params=pltpu.CompilerParams(
+            collective_id=0, has_side_effects=True, vmem_limit_bytes=48 << 20
+        ),
+    )(normed, out_weight)
 
 
 def per_device(
@@ -240,13 +341,7 @@
     y_pack = (y_local + correction).reshape(tok_rows, channels).astype(jnp.bfloat16)
     y_loader = to_loader(y_pack, destination, first_pos, margin)
     normed = gated_norm(y_loader, z_in, norm_gain, groups_here)
-    mixed = lax.psum_scatter(
-        jnp.dot(normed, out_weight, preferred_element_type=jnp.float32).astype(jnp.bfloat16),
-        "head",
-        scatter_dimension=0,
-        tiled=True,
-    )
-    return mixed
+    return project_scatter(normed, out_weight)
 
 
 def solution(mesh):

time: 433 us -> 412 us (0.952)
  waiting for transfers between devices: 127 us -> 48.1 us
  Pallas kernels: 0 us -> 67.3 us
  matrix products: 34.7 us -> 21.8 us
    reduce_scatter x1 -> x0, waiting for transfers between devices: 78.8 us -> none  [per_device(): lax.psum_scatter(jnp.dot(normed, out_weight, preferred_element_type=jnp.f...]
    pallas_call x0 -> x1, Pallas kernels: none -> 67.3 us  [project_scatter(): pl.pallas_call(ring_kernel, out_shape=jax.ShapeDtypeStruct((rows, wide),...]
    dot_general x1 -> x0, matrix products: 12.9 us -> none  [per_device(): jnp.dot(normed, out_weight, preferred_element_type=jnp.float32)]
    unnamed x34 -> x35, local copies, waits for them, and re-layouts: 9.26 us -> 10.1 us
  transfers between devices with their start and end apart: 7 -> 6, of which waited for: 5 -> 4; matrix products, arithmetic and copies ran while one was open for 8% -> 8% of each run, Pallas kernels for 0% -> 0%
where the time goes in v1:
time: 412 us; the launch traced here: 404 us
  local copies, waits for them, and re-layouts  136 us (33%)
  other arithmetic  75.8 us (18%)
  Pallas kernels  67.3 us (16%)
  waiting for transfers between devices  48.1 us (12%)
  matrix products  21.8 us (5%)
  blocking collectives  18.8 us (5%)
  starting transfers between devices  15.2 us (4%)
  between operations  13.8 us (3%)
  loops' own time  7.76 us (2%)
    dynamic_update_slice x6, local copies, waits for them, and re-layouts, per_device(): lax.scan(advance, (empty_state, doc_before), sequence)  85.4 us
    pallas_call x1, Pallas kernels, project_scatter(): pl.pallas_call(ring_kernel, out_shape=jax.ShapeDtypeStruct((rows, wide),...  67.3 us
    all_gather x1, waiting for transfers between devices, prefix(): lax.all_gather(a.astype(kind), axis)  32.1 us
    add x24, other arithmetic, compose(): later[0][..., None, None] * earlier[1] + later[1]  26.7 us
    all_gather x1, blocking collectives, prefix(): lax.all_gather(a.astype(kind), axis)  18.8 us
    unnamed x35, local copies, waits for them, and re-layouts  10.1 us
    dot_general x6, matrix products, ssd_block(): jnp.einsum('ghts,sghp->tghp', mixing, x_block, preferred_element_type=jnp...  9.67 us
    convert_element_type x1, other arithmetic, per_device(): conv_out = jax.nn.silu(conv_sum).astype(jnp.bfloat16)  8.58 us
  transfers between devices with their start and end apart: 6, of which 4 were waited for; matrix products, arithmetic and copies ran while one was open for 8% of the time, Pallas kernels for 0%

profile of v1, /device:TPU:24, one launch (start us, length us, event | category | flops | bytes accessed | tf_op | source)
XLA Modules:
  0.0 404.5 jit_solution(1469645155132841879)
XLA Ops:
  7.4 1.3 compare_select_fusion.1
  8.7 8.0 %scatter_custom_fusion.1 = bf16[769,1296]{1,0:T(8,128)(2,1)S(1)} fusion(s32[768]{0:T(1024)S(1)} %get-tuple-element.334, bf16[]{:T(256)} %constant.145.clone.1, bf16[768,16]{1,0:T(8,128)(2,1)S(1)} %copy.168, bf16[]{:T(256)} %constant.160, bf16[768,256]{1,0:T(8,128)(2,1)} %param.23, bf16[768,1024]{1,0:T(8,128)(2,1)} %param.21), kind=kCustom, calls=%fused_computation.83 | custom fusion | flops 5971968 | bytes 4155940 | tf_op jit(solution)/shard_map/scatter | solution.py:254
  17.9 2.3 copy.171
  20.2 1.9 collective-permute-start
  22.2 1.4 copy.172
  23.6 5.7 %collective-permute-start.1 = (bf16[384,1296]{0,1:T(8,128)(2,1)}, bf16[384,1296]{0,1:T(8,128)(2,1)}, u32[]{:S(2)}, u32[]{:S(2)}) collective-permute-start(bf16[384,1296]{0,1:T(8,128)(2,1)} %copy.172), channel_id=1, source_target_pairs={{8,0},{16,8},{24,16},{32,24},{40,32},{48,40},{56,48},{64,56},{72,6... | collective-permute-start | bytes 2985992 | tf_op jit(solution)/shard_map/ppermute | solution.py:23
  29.3 8.0 %scatter_custom_fusion = bf16[769,1296]{1,0:T(8,128)(2,1)S(1)} fusion(s32[768]{0:T(1024)S(1)} %get-tuple-element.335, bf16[]{:T(256)} %constant.145.clone.1, bf16[768,16]{1,0:T(8,128)(2,1)S(1)} %copy.168, bf16[]{:T(256)} %constant.160, bf16[768,256]{1,0:T(8,128)(2,1)} %param.23, bf16[768,1024]{1,0:T(8,128)(2,1)} %param.21), kind=kCustom, calls=%fused_computation.85 | custom fusion | flops 5971968 | bytes 4155940 | tf_op jit(solution)/shard_map/scatter | solution.py:258
  38.5 1.5 slice.178
  40.9 2.0 copy.195
  43.0 2.7 copy.194
  48.3 1.6 add_dynamic-update-slice_fusion
  49.9 1.7 constant_dynamic-update-slice_fusion
  51.7 2.1 collective-permute-start.2
  54.0 1.4 slice.186
  56.3 6.1 %collective-permute-done.2 = bf16[3,1280]{0,1:T(8,128)(2,1)S(1)} collective-permute-done((bf16[3,1280]{0,1:T(8,128)(2,1)S(1)}, bf16[3,1280]{0,1:T(8,128)(2,1)S(1)}, u32[]{:S(2)}, u32[]{:S(2)}) %collective-permute-start.2) | collective-permute-done | bytes 7712 | tf_op jit(solution)/shard_map/ppermute | solution.py:33
  62.4 8.6 %multiply_convert_fusion.2 = bf16[768,1280]{0,1:T(8,128)(2,1)S(1)} fusion(bf16[768,1280]{0,1:T(8,128)(2,1)} %slice.186, bf16[3,1280]{0,1:T(8,128)(2,1)S(1)} %collective-permute-done.2, f32[1280]{0:T(1024)S(1)} %get-tuple-element.283, f32[768]{0:T(1024)S(1)} %get-tuple-element.337, f32[1280]{0:T(1024)S(1)} %get-tuple-element.284, f32[768]{0:T(1024)S(1)} %copy-done.4, ...), kind=kLoop, calls=%fused_computation.64 | loop fusion | flops 27525120 | bytes 3969536 | tf_op jit(solution)/shard_map/convert_element_type | solution.py:279
  71.1 1.3 slice.194
  72.7 3.4 reshape_reshape.11
  76.1 1.6 copy.177
  77.7 130.2 %while.30 = (s32[]{:T(128)}, f32[1,16,64,128]{3,2,1,0:T(8,128)S(1)}, s32[]{:T(128)}, f32[6,128,1,16,64]{1,0,4,3,2:T(8,128)}, f32[6,128,1,16]{3,1,2,0:T(8,128)}, ...) while((s32[]{:T(128)}, ...), condition=%wide.region_6.7_spmd.clone, body=%wide.region_4.6_spmd.clone.sunk | while | flops 108321296 | bytes 5440525 | solution.py:316
  82.3 1.6 fusion.105
  85.1 14.2 %dynamic_update_slice.6 = f32[6,128,1,16,64]{1,0,4,3,2:T(8,128)} dynamic-update-slice(f32[6,128,1,16,64]{1,0,4,3,2:T(8,128)} %get-tuple-element.463, f32[1,128,1,16,64]{1,0,4,3,2:T(1,128)S(1)} %bitcast.220, s32[]{:T(128)S(6)} %copy.220, s32[]{:T(128)} %constant.138.clone.1..sunk.1, s32[]{:T(128)} %constant.138.clone.1..sunk.1, s32[]{:T(128)} %constant.138.clone.1..sunk.1, s32[]{:T(128)} %constant.138.clone.1..sunk.1) | dynamic-update-slice | bytes 1048580 | tf_op jit(solution)/shard_map/while/body/jit(dynamic_update_index_in_dim)/dynamic_update_slice | solution.py:316
  104.0 1.6 fusion.105
  106.8 14.2 %dynamic_update_slice.6 = f32[6,128,1,16,64]{1,0,4,3,2:T(8,128)} dynamic-update-slice(f32[6,128,1,16,64]{1,0,4,3,2:T(8,128)} %get-tuple-element.463, f32[1,128,1,16,64]{1,0,4,3,2:T(1,128)S(1)} %bitcast.220, s32[]{:T(128)S(6)} %copy.220, s32[]{:T(128)} %constant.138.clone.1..sunk.1, s32[]{:T(128)} %constant.138.clone.1..sunk.1, s32[]{:T(128)} %constant.138.clone.1..sunk.1, s32[]{:T(128)} %constant.138.clone.1..sunk.1) | dynamic-update-slice | bytes 1048580 | tf_op jit(solution)/shard_map/while/body/jit(dynamic_update_index_in_dim)/dynamic_update_slice | solution.py:316
  125.7 1.6 fusion.105
  128.5 14.2 %dynamic_update_slice.6 = f32[6,128,1,16,64]{1,0,4,3,2:T(8,128)} dynamic-update-slice(f32[6,128,1,16,64]{1,0,4,3,2:T(8,128)} %get-tuple-element.463, f32[1,128,1,16,64]{1,0,4,3,2:T(1,128)S(1)} %bitcast.220, s32[]{:T(128)S(6)} %copy.220, s32[]{:T(128)} %constant.138.clone.1..sunk.1, s32[]{:T(128)} %constant.138.clone.1..sunk.1, s32[]{:T(128)} %constant.138.clone.1..sunk.1, s32[]{:T(128)} %constant.138.clone.1..sunk.1) | dynamic-update-slice | bytes 1048580 | tf_op jit(solution)/shard_map/while/body/jit(dynamic_update_index_in_dim)/dynamic_update_slice | solution.py:316
  147.4 1.6 fusion.105
  150.2 14.2 %dynamic_update_slice.6 = f32[6,128,1,16,64]{1,0,4,3,2:T(8,128)} dynamic-update-slice(f32[6,128,1,16,64]{1,0,4,3,2:T(8,128)} %get-tuple-element.463, f32[1,128,1,16,64]{1,0,4,3,2:T(1,128)S(1)} %bitcast.220, s32[]{:T(128)S(6)} %copy.220, s32[]{:T(128)} %constant.138.clone.1..sunk.1, s32[]{:T(128)} %constant.138.clone.1..sunk.1, s32[]{:T(128)} %constant.138.clone.1..sunk.1, s32[]{:T(128)} %constant.138.clone.1..sunk.1) | dynamic-update-slice | bytes 1048580 | tf_op jit(solution)/shard_map/while/body/jit(dynamic_update_index_in_dim)/dynamic_update_slice | solution.py:316
  169.1 1.6 fusion.105
  171.9 14.2 %dynamic_update_slice.6 = f32[6,128,1,16,64]{1,0,4,3,2:T(8,128)} dynamic-update-slice(f32[6,128,1,16,64]{1,0,4,3,2:T(8,128)} %get-tuple-element.463, f32[1,128,1,16,64]{1,0,4,3,2:T(1,128)S(1)} %bitcast.220, s32[]{:T(128)S(6)} %copy.220, s32[]{:T(128)} %constant.138.clone.1..sunk.1, s32[]{:T(128)} %constant.138.clone.1..sunk.1, s32[]{:T(128)} %constant.138.clone.1..sunk.1, s32[]{:T(128)} %constant.138.clone.1..sunk.1) | dynamic-update-slice | bytes 1048580 | tf_op jit(solution)/shard_map/while/body/jit(dynamic_update_index_in_dim)/dynamic_update_slice | solution.py:316
  190.8 1.6 fusion.105
  193.6 14.2 %dynamic_update_slice.6 = f32[6,128,1,16,64]{1,0,4,3,2:T(8,128)} dynamic-update-slice(f32[6,128,1,16,64]{1,0,4,3,2:T(8,128)} %get-tuple-element.463, f32[1,128,1,16,64]{1,0,4,3,2:T(1,128)S(1)} %bitcast.220, s32[]{:T(128)S(6)} %copy.220, s32[]{:T(128)} %constant.138.clone.1..sunk.1, s32[]{:T(128)} %constant.138.clone.1..sunk.1, s32[]{:T(128)} %constant.138.clone.1..sunk.1, s32[]{:T(128)} %constant.138.clone.1..sunk.1) | dynamic-update-slice | bytes 1048580 | tf_op jit(solution)/shard_map/while/body/jit(dynamic_update_index_in_dim)/dynamic_update_slice | solution.py:316
  208.6 1.7 reduce-window.20
  211.0 18.8 %all_gather.10 = bf16[32,1,16]{2,1,0:T(2,128)(2,1)S(1)} all-gather(bf16[1,1,16]{2,1,0:T(2,128)(2,1)S(1)} %copy.184), channel_id=1, replica_groups=mesh['ctx'=32,'head'=8] {'ctx'}, dimensions={0}, use_global_device_ids=true | all-gather | bytes 1056 | tf_op jit(solution)/shard_map/all_gather | solution.py:39
  229.8 4.8 %reshape.383 = f32[768,1,16,64]{0,3,2,1:T(8,128)} reshape(f32[6,128,1,16,64]{1,0,4,3,2:T(8,128)} %get-tuple-element.131) | data formatting | bytes 6291456 | tf_op jit(solution)/shard_map/reshape | solution.py:340
  234.6 32.1 %all-gather.3.cloned.1.call-done = bf16[32,16,64,128]{3,2,1,0:T(8,128)(2,1)} async-done(((bf16[1,16,64,128]{3,2,1,0:T(8,128)(2,1)}), bf16[32,16,64,128]{3,2,1,0:T(8,128)(2,1)}) %all-gather.3.cloned.1.call-update) | async-done | bytes 8388624 | tf_op jit(solution)/shard_map/all_gather | solution.py:39
  266.8 27.6 %while.29 = (s32[]{:T(128)}, f32[1,16,64,128]{3,2,1,0:T(8,128)S(1)}, s32[]{:T(128)}, bf16[32,1,16]{2,1,0:T(2,128)(2,1)S(1)}, bf16[32,1,16,64,128]{4,3,2,1,0:T(8,128)(2,1)}, /*index=5*/s32[]{:T(128)}, s32[]{:T(128)}, s32[]{:T(128)}) while((s32[]{:T(128)}, f32[1,16,64,128]{3,2,1,0:T(8,128)S(1)}, s32[]{:T(128)}, ...), condition=%wide.region_10.11_spmd, body=%wide.region_9.10_spmd.sunk | while | flops 393237 | bytes 1311015 | solution.py:53
  294.4 2.4 fusion.47
  298.1 2.3 copy.186
  301.5 2.2 collective-permute-start.4
  303.7 3.3 collective-permute-start.3
  307.0 1.7 copy.188
  308.7 4.8 %collective-permute-done.4 = bf16[384,1024]{1,0:T(8,128)(2,1)S(1)} collective-permute-done((bf16[384,1024]{1,0:T(8,128)(2,1)}, bf16[384,1024]{1,0:T(8,128)(2,1)S(1)}, u32[]{:S(2)}, u32[]{:S(2)}) %collective-permute-start.4) | collective-permute-done | bytes 786464 | tf_op jit(solution)/shard_map/ppermute | solution.py:23
  314.4 5.1 %collective-permute-done.3 = bf16[384,1024]{1,0:T(8,128)(2,1)} collective-permute-done((bf16[384,1024]{1,0:T(8,128)(2,1)}, bf16[384,1024]{1,0:T(8,128)(2,1)}, u32[]{:S(2)}, u32[]{:S(2)}) %collective-permute-start.3) | collective-permute-done | bytes 786464 | tf_op jit(solution)/shard_map/ppermute | solution.py:21
  319.4 2.1 pad_maximum_fusion
  321.5 3.6 gather_fusion
  325.1 3.1 multiply_reduce_fusion
  329.4 67.3 %shard_map.127 = bf16[96,4096]{1,0:T(8,128)(2,1)S(1)} custom-call(bf16[768,1024]{1,0:T(8,128)(2,1)S(1)} %multiply_convert_fusion.3.normed_ref, bf16[1024,4096]{1,0:T(8,128)(2,1)} %w_hbm.1), custom_call_target="tpu_custom_call" | custom-call | tf_op jit(solution)/shard_map/pallas_call | solution.py:196
  (217 shorter events, 69.8 us)
Async XLA Ops:
  6.5 260.2 %all-gather.3.cloned.1.call-start = ((), (), s32[]{:S(2)}) async-start(), calls=%async_computation | async-start | bytes 8650752 | tf_op jit(solution)/shard_map/all_gather | solution.py:39
  20.2 28.0 %collective-permute-start = (bf16[384,1296]{0,1:T(8,128)(2,1)}, bf16[384,1296]{0,1:T(8,128)(2,1)}, u32[]{:S(2)}, u32[]{:S(2)}) collective-permute-start(bf16[384,1296]{0,1:T(8,128)(2,1)} %copy.171), channel_id=1, source_target_pairs={{0,8},{8,16},{16,24},{24,32},{32,40},{40,48},{48,56},{56,64},{64,7... | collective-permute-start | bytes 2985992 | tf_op jit(solution)/shard_map/ppermute | solution.py:21
  23.6 26.3 %collective-permute-start.1 = (bf16[384,1296]{0,1:T(8,128)(2,1)}, bf16[384,1296]{0,1:T(8,128)(2,1)}, u32[]{:S(2)}, u32[]{:S(2)}) collective-permute-start(bf16[384,1296]{0,1:T(8,128)(2,1)} %copy.172), channel_id=1, source_target_pairs={{8,0},{16,8},{24,16},{32,24},{40,32},{48,40},{56,48},{64,56},{72,6... | collective-permute-start | bytes 2985992 | tf_op jit(solution)/shard_map/ppermute | solution.py:23
  37.4 2.6 copy-start.11
  40.0 5.7 %copy-start.7 = (bf16[4,1024]{1,0:T(4,128)(2,1)S(1)}, bf16[4,1024]{1,0:T(4,128)(2,1)}, u32[]{:S(2)}) copy-start(bf16[4,1024]{1,0:T(4,128)(2,1)} %param.27) | copy-start | bytes 24580
  40.0 5.7 %copy-start.9 = (bf16[4,256]{1,0:T(4,128)(2,1)S(1)}, bf16[4,256]{1,0:T(4,128)(2,1)}, u32[]{:S(2)}) copy-start(bf16[4,256]{1,0:T(4,128)(2,1)} %param.28) | copy-start | bytes 6148
  40.9 6.1 %copy-start.12 = (f32[16]{0:T(128)S(1)}, f32[16]{0:T(128)}, u32[]{:S(2)}) copy-start(f32[16]{0:T(128)} %param.30) | copy-start | bytes 196
  48.3 5.6 %copy-start.10 = (f32[16]{0:T(128)S(1)}, f32[16]{0:T(128)}, u32[]{:S(2)}) copy-start(f32[16]{0:T(128)} %param.29) | copy-start | bytes 196
  51.6 10.9 %copy-start.3 = (f32[1280]{0:T(1024)S(1)}, f32[1280]{0:T(1024)}, u32[]{:S(2)}) copy-start(f32[1280]{0:T(1024)} %get-tuple-element.285) | copy-start | bytes 15364
  51.6 10.9 %copy-start.4 = (f32[768]{0:T(1024)S(1)}, f32[768]{0:T(1024)}, u32[]{:S(2)}) copy-start(f32[768]{0:T(1024)} %get-tuple-element.338) | copy-start | bytes 9220
  51.6 10.9 %copy-start.5 = (f32[768]{0:T(1024)S(1)}, f32[768]{0:T(1024)}, u32[]{:S(2)}) copy-start(f32[768]{0:T(1024)} %get-tuple-element.339) | copy-start | bytes 9220
  51.7 10.7 %collective-permute-start.2 = (bf16[3,1280]{0,1:T(8,128)(2,1)S(1)}, bf16[3,1280]{0,1:T(8,128)(2,1)S(1)}, u32[]{:S(2)}, u32[]{:S(2)}) collective-permute-start(bf16[3,1280]{0,1:T(8,128)(2,1)S(1)} %slice.185), channel_id=1, source_target_pairs={{0,8},{8,16},{16,24},{24,32},{32,40},{40,48},{48,56},{56,64},{64,7... | collective-permute-start | bytes 23048 | tf_op jit(solution)/shard_map/ppermute | solution.py:33
  72.7 5.0 %copy-start.13 = (f32[16]{0:T(128)S(1)}, f32[16]{0:T(128)}, u32[]{:S(2)}) copy-start(f32[16]{0:T(128)} %param.31) | copy-start | bytes 196
  296.9 10.1 %copy-start.8 = (bf16[1024]{0:T(1024)(128)(2,1)S(1)}, bf16[1024]{0:T(1024)(128)(2,1)}, u32[]{:S(2)}) copy-start(bf16[1024]{0:T(1024)(128)(2,1)} %param.32) | copy-start | bytes 6148
  296.9 10.1 %copy-start.6 = (s32[768]{0:T(1024)S(1)}, s32[768]{0:T(1024)}, u32[]{:S(2)}) copy-start(s32[768]{0:T(1024)} %get-tuple-element.333) | copy-start | bytes 9220
  301.5 12.0 %collective-permute-start.4 = (bf16[384,1024]{1,0:T(8,128)(2,1)}, bf16[384,1024]{1,0:T(8,128)(2,1)S(1)}, u32[]{:S(2)}, u32[]{:S(2)}) collective-permute-start(bf16[384,1024]{1,0:T(8,128)(2,1)} %copy.187), channel_id=1, source_target_pairs={{8,0},{16,8},{24,16},{32,24},{40,32},{48,40},{56,48},{64,56},{72,6... | collective-permute-start | bytes 2359304 | tf_op jit(solution)/shard_map/ppermute | solution.py:23
  303.7 15.7 %collective-permute-start.3 = (bf16[384,1024]{1,0:T(8,128)(2,1)}, bf16[384,1024]{1,0:T(8,128)(2,1)}, u32[]{:S(2)}, u32[]{:S(2)}) collective-permute-start(bf16[384,1024]{1,0:T(8,128)(2,1)} %copy.186), channel_id=1, source_target_pairs={{0,8},{8,16},{16,24},{24,32},{32,40},{40,48},{48,56},{56,64},{64,7... | collective-permute-start | bytes 2359304 | tf_op jit(solution)/shard_map/ppermute | solution.py:21
  313.5 0.9 copy-start.2
  325.1 3.1 copy-start
  325.1 3.1 copy-start.1
Sparse Core Ops, SparseCore 0:
  208.8 57.9 all-gather.2

commit v2 on v0

v2 whole, which is shorter than its diff:
```python
import jax
import jax.numpy as jnp
from jax import lax
from jax.experimental import pallas as pl
from jax.experimental.pallas import tpu as pltpu
from jax.sharding import PartitionSpec as P

N = 128
SPAN = 128
KCONV = 4
SUBS = 4
WIDE = 256
TILE = 16
F32 = jnp.float32
BF16 = jnp.bfloat16


def nt(a, b):
    return lax.dot_general(a, b, (((1,), (1,)), ((), ())), preferred_element_type=F32)


def mm(a, b):
    return jnp.dot(a, b, preferred_element_type=F32)


def iota(shape, dim):
    return lax.broadcasted_iota(jnp.int32, shape, dim)


def one_hot(hit):
    return jnp.where(hit, 1.0, 0.0).astype(BF16)


def half_silu(v):
    return 0.5 * v * (1.0 + jnp.tanh(0.5 * v))


def layer_kernel(
    x_hbm,
    z_hbm,
    bc_ref,
    dt_ref,
    dest_ref,
    lengths_ref,
    convx_ref,
    convbc_ref,
    bias_ref,
    alog_ref,
    skip_ref,
    gain_ref,
    w_hbm,
    out_ref,
    x_ref,
    z_ref,
    w_ref,
    pout_ref,
    home_ref,
    q_ref,
    snd,
    rcvp,
    rcvn,
    dts,
    dtr,
    xext,
    conv_ref,
    cols_ref,
    ds_ref,
    car_ref,
    rrow_ref,
    score_ref,
    bt_ref,
    sloc,
    ypart,
    es_ref,
    framed,
    ss_ref,
    normed_ref,
    sa,
    ra,
    ret,
    inc,
    sbuf,
    rbuf,
    x_sems,
    z_sem,
    w_sems,
    xs_sems,
    xr_sems,
    ds_sems,
    dr_sems,
    as_sems,
    ar_sems,
    rs_sems,
    rr_sems,
    ys_sems,
    yr_sems,
    send_sems,
    recv_sems,
):
    nctx = lax.axis_size("ctx")
    nhead = lax.axis_size("head")
    me = lax.axis_index("ctx")
    mz = lax.axis_index("head")
    tok = bc_ref.shape[0]
    margin = tok // 2
    blocks = tok // SPAN
    quads = x_ref.shape[0]
    groups = SPAN // TILE
    heads = dt_ref.shape[1]
    docs = lengths_ref.shape[0]
    first = me * tok
    around = (lax.rem(me + 1, nctx), lax.rem(me + nctx - 1, nctx))
    hops = (lax.rem(mz + 1, nhead), lax.rem(mz + nhead - 1, nhead))

    barrier = pltpu.get_barrier_semaphore()

    def greet(j, _):
        pl.semaphore_signal(barrier, inc=1, device_id={"ctx": lax.rem(me + j, nctx)})
        return 0

    lax.fori_loop(1, nctx, greet, 0)
    for hop in hops:
        pl.semaphore_signal(barrier, inc=1, device_id={"head": hop})

    x_loads = [
        pltpu.make_async_copy(x_hbm.at[:, pl.ds(c * WIDE, WIDE)], x_ref.at[c], x_sems.at[c])
        for c in range(quads)
    ]
    z_load = pltpu.make_async_copy(z_hbm, z_ref, z_sem)
    wide = w_ref.shape[1]
    width = wide // (2 * SUBS)
    w_loads = []
    for sub in range(SUBS):
        for way in range(2):
            w_cols = pl.ds((way * SUBS + sub) * width, width)
            w_loads.append(
                pltpu.make_async_copy(w_hbm.at[:, w_cols], w_ref.at[:, w_cols], w_sems.at[way, sub])
            )
    for load in x_loads:
        load.start()
    z_load.start()
    for load in w_loads:
        load.start()

    rel_row = jnp.concatenate([dest_ref[i : i + 1, :] for i in range(blocks)], axis=1) - first
    slot = iota((margin + TILE, tok), 0)
    goal = jnp.where(slot < margin, slot + tok, slot + (tok - TILE - margin))
    pout_ref[0 : margin + TILE, :] = one_hot(goal == rel_row)
    pout_ref[margin + TILE :, :] = one_hot(iota((margin, tok), 0) - margin == rel_row)

    def exchange(chunk, way):
        if way == 0:
            src, dst = snd.at[chunk, pl.ds(0, margin + TILE)], rcvp.at[chunk]
        else:
            src, dst = snd.at[chunk, pl.ds(margin + TILE, margin)], rcvn.at[chunk]
        return pltpu.make_async_remote_copy(
            src_ref=src,
            dst_ref=dst,
            send_sem=xs_sems.at[chunk, way],
            recv_sem=xr_sems.at[chunk, way],
            device_id={"ctx": around[way]},
        )

    def dt_copy(way):
        return pltpu.make_async_remote_copy(
            src_ref=dts.at[way],
            dst_ref=dtr.at[way],
            send_sem=ds_sems.at[way],
            recv_sem=dr_sems.at[way],
            device_id={"ctx": around[way]},
        )

    def source(chunk):
        return bc_ref[...] if chunk == 0 else x_ref[chunk - 1]

    eye_heads = one_hot(iota((heads, heads), 0) == iota((heads, heads), 1))
    dt_rows = nt(eye_heads, dt_ref[...]).astype(BF16)
    dts[0] = nt(dt_rows, pout_ref[0:margin, :]).astype(BF16)
    dts[1] = nt(dt_rows, pout_ref[margin + TILE :, :]).astype(BF16)
    snd[0] = mm(pout_ref[...], source(0)).astype(BF16)

    pl.semaphore_wait(barrier, nctx + 1)
    for way in range(2):
        dt_copy(way).start()
    for way in range(2):
        exchange(0, way).start()
    for chunk in range(1, quads + 1):
        x_loads[chunk - 1].wait()
        snd[chunk] = mm(pout_ref[...], source(chunk)).astype(BF16)
        for way in range(2):
            exchange(chunk, way).start()

    home_ref[...] = one_hot(iota((tok, tok), 0) == rel_row)

    row16 = iota((heads, SPAN), 0)
    bias = jnp.zeros((heads, SPAN), F32)
    alog = jnp.zeros((heads, SPAN), F32)
    for h in range(heads):
        bias = jnp.where(row16 == h, bias_ref[h], bias)
        alog = jnp.where(row16 == h, alog_ref[h], alog)
    neg_rate = -jnp.exp(alog)
    dt_home = nt(dt_rows, home_ref[...])
    for way in range(2):
        dt_copy(way).wait_recv()
    dt_raw = dt_home + jnp.concatenate([dtr[0].astype(F32), dtr[1].astype(F32)], axis=1)
    steps = []
    rates = []
    for b in range(blocks):
        logit = dt_raw[:, b * SPAN : (b + 1) * SPAN] + bias
        step = jnp.maximum(logit, 0.0) + jnp.log1p(jnp.exp(-jnp.abs(logit)))
        steps.append(step)
        rates.append(step * neg_rate)
    spare = SPAN - blocks * heads
    steps = jnp.concatenate(steps + [jnp.ones((spare, SPAN), F32)], axis=0)
    rates = jnp.concatenate(rates + [jnp.zeros((spare, SPAN), F32)], axis=0)
    row = iota((SPAN, SPAN), 0)
    lane = iota((SPAN, SPAN), 1)
    upper = jnp.where(row <= lane, 1.0, 0.0)
    cum_rows = jnp.dot(
        rates, upper, precision=lax.Precision.HIGHEST, preferred_element_type=F32
    )
    rrow_ref[...] = cum_rows - jnp.log(steps)
    cum = cum_rows.T
    step_cols = steps.T
    shift = heads.bit_length() - 1
    lane_block = lax.shift_right_logical(lane, shift)
    row_block = lax.shift_right_logical(row, shift)
    block_start = first + lane_block * SPAN
    pos = block_start + row
    doc_start = jnp.zeros((SPAN, SPAN), jnp.int32)
    begin = jnp.int32(0)
    for d in range(docs):
        doc_start = jnp.where(pos >= begin, begin, doc_start)
        begin = begin + lengths_ref[d]
    last_start = doc_start[SPAN - 1 : SPAN, :]
    last = cum[SPAN - 1 : SPAN, :]
    same_head = (lane & (heads - 1)) == (row & (heads - 1))
    before = jnp.where(same_head & (row_block < lane_block), 1.0, 0.0)
    offset = jnp.dot(
        jnp.broadcast_to(last, (8, SPAN)),
        before,
        precision=lax.Precision.HIGHEST,
        preferred_element_type=F32,
    )[0:1, :]
    w_cols = jnp.where(pos >= last_start, jnp.exp(last - cum) * step_cols, 0.0)
    entry = jnp.where(doc_start < block_start, jnp.exp(cum), 0.0)
    entry_shard = jnp.where(doc_start < first, jnp.exp(cum + offset), 0.0)
    carried = jnp.where(last_start < block_start[0:1, :], jnp.exp(last), 0.0)
    shard_decay = jnp.where(last_start < first, jnp.exp(last + offset), 0.0)
    carried = jnp.broadcast_to(carried, (8, SPAN))
    for b in range(blocks):
        turn = (SPAN - b * heads) % SPAN
        for kind, array in enumerate((cum, w_cols, entry, entry_shard)):
            cols_ref[kind, b] = pltpu.roll(array, turn, 1) if turn else array
        ds_ref[b] = pltpu.roll(doc_start, turn, 1) if turn else doc_start
        car_ref[b] = pltpu.roll(carried, turn, 1) if turn else carried
    decay_at = (blocks - 1) * heads

    low = iota((1, SPAN), 1) < SPAN // 2

    def spread(cols, quad, at=0):
        parts = []
        for pair in range(2):
            h = at + 4 * quad + 2 * pair
            parts.append(jnp.where(low, cols[:, h : h + 1], cols[:, h + 1 : h + 2]))
        return jnp.concatenate(parts, axis=1)

    def rows_of(b):
        return pl.ds(pl.multiple_of(b * SPAN, SPAN), SPAN)

    def pack_conv(chunk):
        home = mm(home_ref[...], source(chunk))
        for way in range(2):
            exchange(chunk, way).wait_recv()
        xext[0:TILE, :] = rcvp[chunk, margin : margin + TILE, :].astype(F32) + snd[
            chunk, tok : tok + TILE, :
        ].astype(F32)
        xext[TILE : TILE + margin, :] = home[0:margin] + rcvp[chunk, 0:margin, :].astype(F32)
        xext[TILE + margin :, :] = home[margin:] + rcvn[chunk].astype(F32)
        if chunk == 0:
            taps = convbc_ref[...].astype(F32)
        else:
            taps = convx_ref[:, (chunk - 1) * WIDE : chunk * WIDE].astype(F32)

        for b in range(blocks):
            begins = ds_ref[b][:, 0:1] - (first + b * SPAN) - iota((SPAN, 1), 0)
            for half in range(2):
                at = slice(half * SPAN, (half + 1) * SPAN)
                base = b * SPAN + TILE
                total = taps[3:4, at] * xext[base : base + SPAN, at]
                for tap in range(KCONV - 1):
                    back = KCONV - 1 - tap
                    piece = xext[base - back : base - back + SPAN, at]
                    total = total + taps[tap : tap + 1, at] * jnp.where(begins <= -back, piece, 0.0)
                conv_ref[chunk, b * SPAN : (b + 1) * SPAN, at] = half_silu(total).astype(BF16)

    pack_conv(0)

    eye = one_hot(row == lane)

    def prepare(b, _):
        bmat = conv_ref[0, rows_of(b), 0:N]
        cmat = conv_ref[0, rows_of(b), N : 2 * N]
        bt_ref[b] = nt(eye, bmat).astype(BF16)
        begins = ds_ref[b][:, 0:1] - (first + b * SPAN)
        score_ref[b] = jnp.where((lane <= row) & (lane >= begins), nt(cmat, bmat), 0.0)
        return 0

    lax.fori_loop(0, blocks, prepare, 0)

    def state_copy(quad, group, owner, source_id):
        return pltpu.make_async_remote_copy(
            src_ref=sa.at[quad, group],
            dst_ref=ra.at[source_id],
            send_sem=as_sems.at[owner],
            recv_sem=ar_sems.at[source_id],
            device_id={"ctx": owner},
        )

    row16 = iota((TILE, SPAN), 0)
    for quad in range(quads):
        pack_conv(quad + 1)

        def local(b, state, quad=quad):
            sloc[quad, b] = state.astype(BF16)
            weight = spread(cols_ref[1, b], quad)
            weighted = (weight * conv_ref[quad + 1, rows_of(b), :].astype(F32)).astype(BF16)
            return state * spread(car_ref[b][0:1, :], quad) + mm(bt_ref[b], weighted)

        state = lax.fori_loop(0, blocks, local, jnp.zeros((N, WIDE), F32))
        sa[quad, :, :, 0:WIDE] = state.astype(BF16).reshape(groups, TILE, WIDE)
        decay = spread(shard_decay, quad, decay_at)
        decay = jnp.where(row16 < TILE // 2, decay[:, 0:SPAN], decay[:, SPAN:])
        rough = decay.astype(BF16).astype(F32)
        decay = jnp.where((row16 & (TILE // 4)) == 0, rough, decay - rough).astype(BF16)
        for group in range(groups):
            sa[quad, group, :, WIDE:] = decay

        def give(j, _, quad=quad):
            group = lax.rem(j + me, groups)
            owner = group * quads + quad

            @pl.when(owner != me)
            def _():
                state_copy(quad, group, owner, me).start()

            @pl.when(owner == me)
            def _():
                ra[me] = sa[quad, group]

            return 0

        lax.fori_loop(0, groups, give, 0)

    def inner(quad):
        def block(b, _):
            xs = conv_ref[quad + 1, rows_of(b), :]
            cmat = conv_ref[0, rows_of(b), N : 2 * N]
            cum_cols = cols_ref[0, b]
            gaps = rrow_ref[pl.ds(pl.multiple_of(b * heads, heads), heads), :]
            score = score_ref[b]
            x_float = xs.astype(F32)
            y = mm(cmat, sloc[quad, b]) * spread(cols_ref[2, b], quad)
            parts = []
            for pair in range(2):
                mixing = []
                for h in (4 * quad + 2 * pair, 4 * quad + 2 * pair + 1):
                    gap = jnp.minimum(cum_cols[:, h : h + 1] - gaps[h : h + 1, :], 60.0)
                    mixing.append((jnp.exp(gap) * score).astype(BF16))
                x_pair = x_float[:, pair * SPAN : (pair + 1) * SPAN]
                x_both = jnp.concatenate(
                    [jnp.where(low, x_pair, 0.0), jnp.where(low, 0.0, x_pair)], axis=0
                ).astype(BF16)
                h = 4 * quad + 2 * pair
                skip = jnp.where(low, skip_ref[h], skip_ref[h + 1])
                parts.append(mm(jnp.concatenate(mixing, axis=1), x_both) + skip * x_pair)
            ypart[quad, rows_of(b), :] = y + jnp.concatenate(parts, axis=1)
            es_ref[quad, rows_of(b), :] = spread(cols_ref[3, b], quad)
            return 0

        lax.fori_loop(0, blocks, block, 0)

    for quad in range(quads // 2):
        inner(quad)

    my_quad = lax.rem(me, quads)
    my_group = lax.div(me, quads)

    def back_copy(shard, quad, group, owner):
        return pltpu.make_async_remote_copy(
            src_ref=ret.at[shard],
            dst_ref=inc.at[quad, group],
            send_sem=rs_sems.at[shard],
            recv_sem=rr_sems.at[owner],
            device_id={"ctx": shard},
        )

    def scan(shard, state):
        ret[shard] = state.astype(BF16)

        @pl.when(shard != me)
        def _():
            back_copy(shard, my_quad, my_group, me).start()
            state_copy(0, 0, 0, shard).wait_recv()

        @pl.when(shard == me)
        def _():
            inc[my_quad, my_group] = state.astype(BF16)

        held = ra[shard].astype(F32)
        quarter = TILE // 4
        decay = jnp.concatenate(
            [
                held[0:1, WIDE:] + held[quarter : quarter + 1, WIDE:],
                held[2 * quarter : 2 * quarter + 1, WIDE:]
                + held[3 * quarter : 3 * quarter + 1, WIDE:],
            ],
            axis=1,
        )
        return state * decay + held[:, 0:WIDE]

    lax.fori_loop(0, nctx, scan, jnp.zeros((TILE, WIDE), F32))

    for quad in range(quads // 2, quads):
        inner(quad)

    def y_copy(quad, way):
        if way == 0:
            src, dst = pl.ds(2 * margin, margin), pl.ds(0, margin)
        else:
            src, dst = pl.ds(margin, margin), pl.ds(3 * margin, margin)
        return pltpu.make_async_remote_copy(
            src_ref=framed.at[quad, src],
            dst_ref=framed.at[quad, dst],
            send_sem=ys_sems.at[quad, way],
            recv_sem=yr_sems.at[quad, way],
            device_id={"ctx": around[way]},
        )

    for quad in range(quads):

        def arrive(group, _, quad=quad):
            owner = group * quads + quad

            @pl.when(owner != me)
            def _():
                back_copy(0, quad, group, owner).wait_recv()

            return 0

        lax.fori_loop(0, groups, arrive, 0)
        incoming = inc[quad].reshape(N, WIDE)
        fix = mm(conv_ref[0, :, N : 2 * N], incoming)
        framed[quad, margin : margin + tok, :] = (ypart[quad] + fix * es_ref[quad]).astype(BF16)
        for way in range(2):
            y_copy(quad, way).start()

    for i in range(blocks):
        across = jnp.broadcast_to(dest_ref[i : i + 1, :], (SPAN, SPAN)).T - first + margin
        for j in range(2 * blocks):
            q_ref[i * SPAN : (i + 1) * SPAN, j * SPAN : (j + 1) * SPAN] = one_hot(
                across == lane + j * SPAN
            )
    z_load.wait()
    for quad in range(quads):
        for way in range(2):
            y_copy(quad, way).wait_recv()
        y_rows = mm(q_ref[...], framed[quad])
        z_cols = z_ref[:, quad * WIDE : (quad + 1) * WIDE].astype(F32)
        gated = y_rows * half_silu(z_cols)
        ypart[quad] = gated
        square = gated * gated
        square = square[:, 0:SPAN] + square[:, SPAN:]
        ss_ref[...] = square if quad == 0 else ss_ref[...] + square

    def norm(i, _):
        inv = lax.rsqrt(
            jnp.sum(ss_ref[rows_of(i), :], axis=1, keepdims=True) * (1.0 / (quads * WIDE)) + 1e-05
        )
        for quad in range(quads):
            at = slice(quad * WIDE, (quad + 1) * WIDE)
            gain = gain_ref[:, at].astype(F32)
            normed_ref[rows_of(i), at] = (ypart[quad, rows_of(i), :] * inv * gain).astype(BF16)
        return 0

    lax.fori_loop(0, blocks, norm, 0)

    rows = out_ref.shape[0]
    rbuf[0] = jnp.zeros_like(rbuf[0])
    for load in w_loads:
        load.wait()

    def ring(step, way, sub):
        return pltpu.make_async_remote_copy(
            src_ref=sbuf.at[step, way, sub],
            dst_ref=rbuf.at[step + 1, way, sub],
            send_sem=send_sems.at[step, way, sub],
            recv_sem=recv_sems.at[step, way, sub],
            device_id={"head": hops[way]},
        )

    def one(step, _):
        for sub in range(SUBS):
            for way in range(2):
                if way == 0:
                    chunk = lax.rem(mz + 2 * nhead - 1 - step, nhead)
                else:
                    chunk = lax.rem(mz + 1 + step, nhead)
                at = (way * SUBS + sub) * width
                part = mm(
                    normed_ref[pl.ds(pl.multiple_of(chunk * rows, rows), rows), :],
                    w_ref[:, at : at + width],
                )

                @pl.when(step > 0)
                def _():
                    ring(step - 1, way, sub).wait_recv()

                total = (part + rbuf[step, way, sub].astype(F32)).astype(BF16)

                @pl.when(step < nhead - 1)
                def _():
                    sbuf[step, way, sub] = total
                    ring(step, way, sub).start()

                @pl.when(step == nhead - 1)
                def _():
                    out_ref[:, at : at + width] = total

        return 0

    lax.fori_loop(0, nhead, one, 0)

    def drain(step, _):
        for sub in range(SUBS):
            for way in range(2):
                ring(step, way, sub).wait_send()
        return 0

    lax.fori_loop(0, nhead - 1, drain, 0)
    for way in range(2):
        dt_copy(way).wait_send()
        for chunk in range(quads + 1):
            exchange(chunk, way).wait_send()
        for quad in range(quads):
            y_copy(quad, way).wait_send()

    def drain_states(other, _):
        @pl.when(other != me)
        def _():
            state_copy(0, 0, other, 0).wait_send()
            back_copy(other, 0, 0, 0).wait_send()

        return 0

    lax.fori_loop(0, nctx, drain_states, 0)


def per_device(
    x_in,
    z_in,
    bc_in,
    dt_in,
    destination,
    doc_lengths,
    conv_x,
    conv_bc,
    dt_bias,
    a_log,
    skip_gain,
    norm_gain,
    out_weight,
):
    nctx = lax.axis_size("ctx")
    nhead = lax.axis_size("head")
    tok, channels = x_in.shape
    heads = dt_in.shape[1]
    margin = tok // 2
    blocks = tok // SPAN
    quads = channels // WIDE
    groups = N // TILE
    rows = tok // nhead
    depth, wide = out_weight.shape
    width = wide // (2 * SUBS)
    dma = pltpu.SemaphoreType.DMA
    vmem = pl.BlockSpec(memory_space=pltpu.VMEM)
    smem = pl.BlockSpec(memory_space=pltpu.SMEM)
    anywhere = pl.BlockSpec(memory_space=pl.ANY)
    scratch = [
        pltpu.VMEM((quads, tok, WIDE), BF16),
        pltpu.VMEM((tok, channels), BF16),
        pltpu.VMEM((depth, wide), BF16),
        pltpu.VMEM((tok + TILE, tok), BF16),
        pltpu.VMEM((tok, tok), BF16),
        pltpu.VMEM((tok, 2 * tok), BF16),
        pltpu.VMEM((quads + 1, tok + TILE, WIDE), BF16),
        pltpu.VMEM((quads + 1, margin + TILE, WIDE), BF16),
        pltpu.VMEM((quads + 1, margin, WIDE), BF16),
        pltpu.VMEM((2, heads, margin), BF16),
        pltpu.VMEM((2, heads, margin), BF16),
        pltpu.VMEM((tok + TILE, WIDE), F32),
        pltpu.VMEM((quads + 1, tok, WIDE), BF16),
        pltpu.VMEM((4, blocks, SPAN, SPAN), F32),
        pltpu.VMEM((blocks, SPAN, SPAN), jnp.int32),
        pltpu.VMEM((blocks, 8, SPAN), F32),
        pltpu.VMEM((SPAN, SPAN), F32),
        pltpu.VMEM((blocks, SPAN, SPAN), F32),
        pltpu.VMEM((blocks, N, SPAN), BF16),
        pltpu.VMEM((quads, blocks, N, WIDE), BF16),
        pltpu.VMEM((quads, tok, WIDE), F32),
        pltpu.VMEM((quads, tok, WIDE), F32),
        pltpu.VMEM((quads, 2 * tok, WIDE), BF16),
        pltpu.VMEM((tok, SPAN), F32),
        pltpu.VMEM((tok, channels), BF16),
        pltpu.VMEM((quads, groups, TILE, WIDE + SPAN), BF16),
        pltpu.VMEM((nctx, TILE, WIDE + SPAN), BF16),
        pltpu.VMEM((nctx, TILE, WIDE), BF16),
        pltpu.VMEM((quads, groups, TILE, WIDE), BF16),
        pltpu.VMEM((nhead - 1, 2, SUBS, rows, width), BF16),
        pltpu.VMEM((nhead, 2, SUBS, rows, width), BF16),
        dma((quads,)),
        dma(()),
        dma((2, SUBS)),
        dma((quads + 1, 2)),
        dma((quads + 1, 2)),
        dma((2,)),
        dma((2,)),
        dma((nctx,)),
        dma((nctx,)),
        dma((nctx,)),
        dma((nctx,)),
        dma((quads, 2)),
        dma((quads, 2)),
        dma((nhead - 1, 2, SUBS)),
        dma((nhead - 1, 2, SUBS)),
    ]
    return pl.pallas_call(
        layer_kernel,
        out_shape=jax.ShapeDtypeStruct((rows, wide), BF16),
        in_specs=[
            anywhere,
            anywhere,
            vmem,
            vmem,
            vmem,
            smem,
            vmem,
            vmem,
            smem,
            smem,
            smem,
            vmem,
            anywhere,
        ],
        out_specs=vmem,
        scratch_shapes=scratch,
        compiler_params=pltpu.CompilerParams(
            collective_id=0, has_side_effects=True, vmem_limit_bytes=60 << 20
        ),
    )(
        x_in,
        z_in,
        bc_in,
        dt_in,
        destination.reshape(blocks, SPAN),
        doc_lengths,
        conv_x,
        conv_bc,
        dt_bias,
        a_log,
        skip_gain,
        norm_gain.reshape(1, channels),
        out_weight,
    )


def solution(mesh):
    placed = (
        P("ctx", "head"),
        P("ctx", "head"),
        P("ctx", "head"),
        P("ctx", "head"),
        P("ctx"),
        P(),
        P(None, "head"),
        P(None, "head"),
        P("head"),
        P("head"),
        P("head"),
        P("head"),
        P("head", None),
    )
    return jax.shard_map(
        per_device, mesh=mesh, in_specs=placed, out_specs=P(("ctx", "head"), None), check_vma=False
    )
```

time: 433 us -> 126 us (0.29); the launches traced: 427 us -> 125 us
  local copies, waits for them, and re-layouts: 135 us -> 4.89 us
  waiting for transfers between devices: 127 us -> 0 us
  Pallas kernels: 0 us -> 120 us
  other arithmetic: 74.7 us -> 0 us
  matrix products: 34.7 us -> 0 us
  blocking collectives: 18.8 us -> 0 us
  starting transfers between devices: 15.2 us -> 0 us
  between operations: 13.8 us -> 0.01 us
  loops' own time: 7.76 us -> 0 us
    pallas_call x0 -> x1, Pallas kernels: none -> 120 us  [per_device(): pl.pallas_call(layer_kernel, out_shape=jax.ShapeDtypeStruct((rows, wide),...]
    dynamic_update_slice x6 -> x0, local copies, waits for them, and re-layouts: 85.4 us -> none  [per_device(): lax.scan(advance, (empty_state, doc_before), sequence)]
    reduce_scatter x1 -> x0, waiting for transfers between devices: 78.8 us -> none  [per_device(): lax.psum_scatter(jnp.dot(normed, out_weight, preferred_element_type=jnp.f...]
    dot_general x26 -> x0, matrix products: 34.7 us -> none  [the longest x1 12.9 us: per_device(): jnp.dot(normed, out_weight, preferred_element_type=jnp.float32)]
    all_gather x1 -> x0, waiting for transfers between devices: 32 us -> none  [prefix(): lax.all_gather(a.astype(kind), axis)]
    add x25 -> x0, other arithmetic: 26.7 us -> none  [the longest x24 26.7 us: compose(): later[0][..., None, None] * earlier[1] + later[1]]
    all_gather x1 -> x0, blocking collectives: 18.8 us -> none  [prefix(): lax.all_gather(a.astype(kind), axis)]
    slice x23 -> x0, local copies, waits for them, and re-layouts: 18.8 us -> none  [the longest x3 5.77 us: padded(): lax.slice_in_dim(cells, cells.shape[dim] - width, cells.shape[dim], axis=...]
  transfers between devices with their start and end apart: 7 -> 0, of which waited for: 5 -> 0; matrix products, arithmetic and copies ran while one was open for 8% -> 0% of each run, Pallas kernels for 0% -> 0%
where the time goes in v2:
time: 126 us; the launch traced here: 125 us
  Pallas kernels  120 us (95%)
  local copies, waits for them, and re-layouts  4.89 us (4%)
    pallas_call x1, Pallas kernels, per_device(): pl.pallas_call(layer_kernel, out_shape=jax.ShapeDtypeStruct((rows, wide),...  120 us
    unnamed x2, local copies, waits for them, and re-layouts  3.61 us

profile of v2, /device:TPU:24, one launch (start us, length us, event | category | flops | bytes accessed | tf_op | source)
XLA Modules:
  0.0 125.3 jit_solution(8555170386575438105)
XLA Ops:
  0.0 1.3 %reshape.7.gain_ref = bf16[1,1024]{1,0:T(2,128)(2,1)} reshape(bf16[1024]{0:T(1024)(128)(2,1)} %param.24) | data formatting | bytes 4096 | tf_op jit(solution)/shard_map/reshape | solution.py:672
  1.3 1.6 %copy.14.dt_ref = bf16[768,16]{1,0:T(8,128)(2,1)} copy(bf16[768,16]{0,1:T(8,128)(2,1)} %param.16) | data formatting | bytes 49152 | tf_op args[3]
  2.8 120.4 %shard_map.127 = bf16[96,4096]{1,0:T(8,128)(2,1)} custom-call(bf16[768,1024]{1,0:T(8,128)(2,1)} %x_hbm.1, bf16[768,1024]{1,0:T(8,128)(2,1)} %z_hbm.1, bf16[768,256]{1,0:T(8,128)(2,1)} %bc_ref.1, bf16[768,16]{1,0:T(8,128)(2,1)} %copy.14.dt_ref, s32[6,128]{1,0:T(8,128)} %bitcast.1, s32[16]{0:T(128)} %lengths_ref.1, bf16[4,1024]{1,0:T(4,128)(2,1)} %convx_ref.1, ...), custom_call_target="tpu_custom_call" | custom-call | tf_op jit(solution)/shard_map/pallas_call | solution.py:637
  123.2 2.1 %copy.16 = bf16[96,4096]{1,0:T(8,128)(2,1)} copy(bf16[96,4096]{1,0:T(8,128)(2,1)} %shard_map.127) | data formatting | bytes 1572864

commit v3 on v2

--- a/solution.py
+++ b/solution.py
@@ -11,6 +11,7 @@
 SUBS = 4
 WIDE = 256
 TILE = 16
+LOG2E = 1.4426950408889634
 F32 = jnp.float32
 BF16 = jnp.bfloat16
 
@@ -32,13 +33,18 @@
 
 
 def half_silu(v):
-    return 0.5 * v * (1.0 + jnp.tanh(0.5 * v))
+    half = 0.5 * v
+    return half + half * jnp.tanh(half)
+
+
+def scope(name):
+    return jax.named_scope(name)
 
 
 def layer_kernel(
     x_hbm,
     z_hbm,
-    bc_ref,
+    bc_hbm,
     dt_ref,
     dest_ref,
     lengths_ref,
@@ -50,20 +56,25 @@
     gain_ref,
     w_hbm,
     out_ref,
+    bc_ref,
     x_ref,
     z_ref,
     w_ref,
     pout_ref,
     home_ref,
-    q_ref,
+    qhome_ref,
+    qaway_ref,
     snd,
     rcvp,
     rcvn,
     dts,
     dtr,
     xext,
+    mask_ref,
     conv_ref,
     cols_ref,
+    part_ref,
+    head_ref,
     ds_ref,
     car_ref,
     rrow_ref,
@@ -72,15 +83,19 @@
     sloc,
     ypart,
     es_ref,
-    framed,
+    y_home,
+    y_away,
     ss_ref,
     normed_ref,
     sa,
     ra,
+    da,
+    rd,
     ret,
     inc,
     sbuf,
     rbuf,
+    bc_sem,
     x_sems,
     z_sem,
     w_sems,
@@ -90,6 +105,8 @@
     dr_sems,
     as_sems,
     ar_sems,
+    ads_sems,
+    adr_sems,
     rs_sems,
     rr_sems,
     ys_sems,
@@ -106,7 +123,7 @@
     blocks = tok // SPAN
     quads = x_ref.shape[0]
     groups = SPAN // TILE
-    heads = dt_ref.shape[1]
+    heads = dt_ref.shape[0]
     docs = lengths_ref.shape[0]
     first = me * tok
     around = (lax.rem(me + 1, nctx), lax.rem(me + nctx - 1, nctx))
@@ -122,6 +139,8 @@
     for hop in hops:
         pl.semaphore_signal(barrier, inc=1, device_id={"head": hop})
 
+    bc_load = pltpu.make_async_copy(bc_hbm, bc_ref, bc_sem)
+    bc_load.start()
     x_loads = [
         pltpu.make_async_copy(x_hbm.at[:, pl.ds(c * WIDE, WIDE)], x_ref.at[c], x_sems.at[c])
         for c in range(quads)
@@ -136,11 +155,6 @@
             w_loads.append(
                 pltpu.make_async_copy(w_hbm.at[:, w_cols], w_ref.at[:, w_cols], w_sems.at[way, sub])
             )
-    for load in x_loads:
-        load.start()
-    z_load.start()
-    for load in w_loads:
-        load.start()
 
     rel_row = jnp.concatenate([dest_ref[i : i + 1, :] for i in range(blocks)], axis=1) - first
     slot = iota((margin + TILE, tok), 0)
@@ -173,10 +187,12 @@
     def source(chunk):
         return bc_ref[...] if chunk == 0 else x_ref[chunk - 1]
 
-    eye_heads = one_hot(iota((heads, heads), 0) == iota((heads, heads), 1))
-    dt_rows = nt(eye_heads, dt_ref[...]).astype(BF16)
+    dt_rows = dt_ref[...]
     dts[0] = nt(dt_rows, pout_ref[0:margin, :]).astype(BF16)
     dts[1] = nt(dt_rows, pout_ref[margin + TILE :, :]).astype(BF16)
+    bc_load.wait()
+    for load in x_loads:
+        load.start()
     snd[0] = mm(pout_ref[...], source(0)).astype(BF16)
 
     pl.semaphore_wait(barrier, nctx + 1)
@@ -190,6 +206,10 @@
         for way in range(2):
             exchange(chunk, way).start()
 
+    z_load.start()
+    for load in w_loads:
+        load.start()
+
     home_ref[...] = one_hot(iota((tok, tok), 0) == rel_row)
 
     row16 = iota((heads, SPAN), 0)
@@ -199,9 +219,10 @@
         bias = jnp.where(row16 == h, bias_ref[h], bias)
         alog = jnp.where(row16 == h, alog_ref[h], alog)
     neg_rate = -jnp.exp(alog)
-    dt_home = nt(dt_rows, home_ref[...])
     for way in range(2):
         dt_copy(way).wait_recv()
+    dt_home = nt(dt_rows, home_ref[...])
+    home_first = mm(home_ref[...], source(0))
     dt_raw = dt_home + jnp.concatenate([dtr[0].astype(F32), dtr[1].astype(F32)], axis=1)
     steps = []
     rates = []
@@ -219,7 +240,7 @@
     cum_rows = jnp.dot(
         rates, upper, precision=lax.Precision.HIGHEST, preferred_element_type=F32
     )
-    rrow_ref[...] = cum_rows - jnp.log(steps)
+    rrow_ref[...] = LOG2E * (cum_rows - jnp.log(steps))
     cum = cum_rows.T
     step_cols = steps.T
     shift = heads.bit_length() - 1
@@ -250,10 +271,19 @@
     carried = jnp.broadcast_to(carried, (8, SPAN))
     for b in range(blocks):
         turn = (SPAN - b * heads) % SPAN
-        for kind, array in enumerate((cum, w_cols, entry, entry_shard)):
-            cols_ref[kind, b] = pltpu.roll(array, turn, 1) if turn else array
+        cols_ref[b] = pltpu.roll(LOG2E * cum, turn, 1) if turn else LOG2E * cum
+        for kind, array in enumerate((w_cols, entry, entry_shard)):
+            array = pltpu.roll(array, turn, 1) if turn else array
+            rough = array.astype(BF16)
+            fine = (array - rough.astype(F32)).astype(BF16)
+            part_ref[kind, b * SPAN : (b + 1) * SPAN, 0:SPAN] = rough
+            part_ref[kind, b * SPAN : (b + 1) * SPAN, SPAN:] = fine
         ds_ref[b] = pltpu.roll(doc_start, turn, 1) if turn else doc_start
         car_ref[b] = pltpu.roll(carried, turn, 1) if turn else carried
+    for quad in range(quads):
+        key = iota((2 * SPAN, WIDE), 0) & (SPAN - 1)
+        head = lax.shift_right_logical(iota((2 * SPAN, WIDE), 1), 6) + 4 * quad
+        head_ref[quad] = one_hot(key == head)
     decay_at = (blocks - 1) * heads
 
     low = iota((1, SPAN), 1) < SPAN // 2
@@ -268,33 +298,44 @@
     def rows_of(b):
         return pl.ds(pl.multiple_of(b * SPAN, SPAN), SPAN)
 
-    def pack_conv(chunk):
-        home = mm(home_ref[...], source(chunk))
+    def pack_conv(chunk, home=None):
+        if home is None:
+            home = mm(home_ref[...], source(chunk))
         for way in range(2):
             exchange(chunk, way).wait_recv()
-        xext[0:TILE, :] = rcvp[chunk, margin : margin + TILE, :].astype(F32) + snd[
-            chunk, tok : tok + TILE, :
-        ].astype(F32)
-        xext[TILE : TILE + margin, :] = home[0:margin] + rcvp[chunk, 0:margin, :].astype(F32)
-        xext[TILE + margin :, :] = home[margin:] + rcvn[chunk].astype(F32)
         if chunk == 0:
             taps = convbc_ref[...].astype(F32)
         else:
             taps = convx_ref[:, (chunk - 1) * WIDE : chunk * WIDE].astype(F32)
-
-        for b in range(blocks):
-            begins = ds_ref[b][:, 0:1] - (first + b * SPAN) - iota((SPAN, 1), 0)
+        for half in range(2):
+            at = slice(half * SPAN, (half + 1) * SPAN)
+            xext[half, 0:TILE, :] = rcvp[chunk, margin : margin + TILE, at].astype(F32) + snd[
+                chunk, tok : tok + TILE, at
+            ].astype(F32)
+            xext[half, TILE : TILE + margin, :] = home[0:margin, at] + rcvp[
+                chunk, 0:margin, at
+            ].astype(F32)
+            xext[half, TILE + margin :, :] = home[margin:, at] + rcvn[chunk, :, at].astype(F32)
+        with scope("conv"):
             for half in range(2):
                 at = slice(half * SPAN, (half + 1) * SPAN)
-                base = b * SPAN + TILE
-                total = taps[3:4, at] * xext[base : base + SPAN, at]
-                for tap in range(KCONV - 1):
-                    back = KCONV - 1 - tap
-                    piece = xext[base - back : base - back + SPAN, at]
-                    total = total + taps[tap : tap + 1, at] * jnp.where(begins <= -back, piece, 0.0)
-                conv_ref[chunk, b * SPAN : (b + 1) * SPAN, at] = half_silu(total).astype(BF16)
-
-    pack_conv(0)
+                for b in range(blocks):
+                    base = b * SPAN + TILE
+                    total = taps[3:4, at] * xext[half, base : base + SPAN, :]
+                    for tap in range(KCONV - 1):
+                        back = KCONV - 1 - tap
+                        piece = xext[half, base - back : base - back + SPAN, :]
+                        usable = mask_ref[tap, b * SPAN : (b + 1) * SPAN, :]
+                        total = total + taps[tap : tap + 1, at] * (usable * piece)
+                    conv_ref[chunk, b * SPAN : (b + 1) * SPAN, at] = half_silu(total).astype(BF16)
+
+    for b in range(blocks):
+        begins = jnp.broadcast_to(ds_ref[b][:, 0:1], (SPAN, SPAN)) - (first + b * SPAN) - row
+        for tap in range(KCONV - 1):
+            usable = jnp.where(begins <= tap + 1 - KCONV, 1.0, 0.0)
+            mask_ref[tap, b * SPAN : (b + 1) * SPAN, :] = usable
+
+    pack_conv(0, home_first)
 
     eye = one_hot(row == lane)
 
@@ -306,7 +347,7 @@
         score_ref[b] = jnp.where((lane <= row) & (lane >= begins), nt(cmat, bmat), 0.0)
         return 0
 
-    lax.fori_loop(0, blocks, prepare, 0)
+    lax.fori_loop(0, blocks, prepare, 0, unroll=True)
 
     def state_copy(quad, group, owner, source_id):
         return pltpu.make_async_remote_copy(
@@ -317,56 +358,64 @@
             device_id={"ctx": owner},
         )
 
-    row16 = iota((TILE, SPAN), 0)
-    for quad in range(quads):
-        pack_conv(quad + 1)
-
-        def local(b, state, quad=quad):
+    def decay_copy(quad, owner, source_id):
+        return pltpu.make_async_remote_copy(
+            src_ref=da.at[quad, pl.ds(0, 1)],
+            dst_ref=rd.at[source_id, pl.ds(0, 1)],
+            send_sem=ads_sems.at[owner],
+            recv_sem=adr_sems.at[source_id],
+            device_id={"ctx": owner},
+        )
+
+    def shard_state(quad):
+        weights = mm(part_ref[0], head_ref[quad])
+        state = jnp.zeros((N, WIDE), F32)
+        for b in range(blocks):
             sloc[quad, b] = state.astype(BF16)
-            weight = spread(cols_ref[1, b], quad)
-            weighted = (weight * conv_ref[quad + 1, rows_of(b), :].astype(F32)).astype(BF16)
-            return state * spread(car_ref[b][0:1, :], quad) + mm(bt_ref[b], weighted)
-
-        state = lax.fori_loop(0, blocks, local, jnp.zeros((N, WIDE), F32))
-        sa[quad, :, :, 0:WIDE] = state.astype(BF16).reshape(groups, TILE, WIDE)
-        decay = spread(shard_decay, quad, decay_at)
-        decay = jnp.where(row16 < TILE // 2, decay[:, 0:SPAN], decay[:, SPAN:])
-        rough = decay.astype(BF16).astype(F32)
-        decay = jnp.where((row16 & (TILE // 4)) == 0, rough, decay - rough).astype(BF16)
-        for group in range(groups):
-            sa[quad, group, :, WIDE:] = decay
-
-        def give(j, _, quad=quad):
+            weight = weights[b * SPAN : (b + 1) * SPAN]
+            x_float = conv_ref[quad + 1, b * SPAN : (b + 1) * SPAN, :].astype(F32)
+            inner_sum = mm(bt_ref[b], (weight * x_float).astype(BF16))
+            state = state * spread(car_ref[b][0:1, :], quad) + inner_sum
+
+        sa[quad] = state.astype(BF16).reshape(groups, TILE, WIDE)
+        da[quad] = jnp.broadcast_to(spread(shard_decay, quad, decay_at), (8, WIDE))
+
+        def give(j, _):
             group = lax.rem(j + me, groups)
             owner = group * quads + quad
 
             @pl.when(owner != me)
             def _():
                 state_copy(quad, group, owner, me).start()
+                decay_copy(quad, owner, me).start()
 
             @pl.when(owner == me)
             def _():
                 ra[me] = sa[quad, group]
+                rd[me] = da[quad]
 
             return 0
 
         lax.fori_loop(0, groups, give, 0)
 
     def inner(quad):
-        def block(b, _):
+        entries = mm(part_ref[1], head_ref[quad])
+        es_ref[quad] = mm(part_ref[2], head_ref[quad])
+
+        for b in range(blocks):
             xs = conv_ref[quad + 1, rows_of(b), :]
             cmat = conv_ref[0, rows_of(b), N : 2 * N]
-            cum_cols = cols_ref[0, b]
-            gaps = rrow_ref[pl.ds(pl.multiple_of(b * heads, heads), heads), :]
+            cum_cols = cols_ref[b]
+            gaps = rrow_ref[b * heads : (b + 1) * heads, :]
             score = score_ref[b]
             x_float = xs.astype(F32)
-            y = mm(cmat, sloc[quad, b]) * spread(cols_ref[2, b], quad)
+            y = mm(cmat, sloc[quad, b]) * entries[b * SPAN : (b + 1) * SPAN]
             parts = []
             for pair in range(2):
                 mixing = []
                 for h in (4 * quad + 2 * pair, 4 * quad + 2 * pair + 1):
-                    gap = jnp.minimum(cum_cols[:, h : h + 1] - gaps[h : h + 1, :], 60.0)
-                    mixing.append((jnp.exp(gap) * score).astype(BF16))
+                    gap = jnp.minimum(cum_cols[:, h : h + 1] - gaps[h : h + 1, :], 80.0)
+                    mixing.append((jnp.exp2(gap) * score).astype(BF16))
                 x_pair = x_float[:, pair * SPAN : (pair + 1) * SPAN]
                 x_both = jnp.concatenate(
                     [jnp.where(low, x_pair, 0.0), jnp.where(low, 0.0, x_pair)], axis=0
@@ -375,13 +424,6 @@
                 skip = jnp.where(low, skip_ref[h], skip_ref[h + 1])
                 parts.append(mm(jnp.concatenate(mixing, axis=1), x_both) + skip * x_pair)
             ypart[quad, rows_of(b), :] = y + jnp.concatenate(parts, axis=1)
-            es_ref[quad, rows_of(b), :] = spread(cols_ref[3, b], quad)
-            return 0
-
-        lax.fori_loop(0, blocks, block, 0)
-
-    for quad in range(quads // 2):
-        inner(quad)
 
     my_quad = lax.rem(me, quads)
     my_group = lax.div(me, quads)
@@ -402,44 +444,34 @@
         def _():
             back_copy(shard, my_quad, my_group, me).start()
             state_copy(0, 0, 0, shard).wait_recv()
+            decay_copy(0, 0, shard).wait_recv()
 
         @pl.when(shard == me)
         def _():
             inc[my_quad, my_group] = state.astype(BF16)
 
-        held = ra[shard].astype(F32)
-        quarter = TILE // 4
-        decay = jnp.concatenate(
-            [
-                held[0:1, WIDE:] + held[quarter : quarter + 1, WIDE:],
-                held[2 * quarter : 2 * quarter + 1, WIDE:]
-                + held[3 * quarter : 3 * quarter + 1, WIDE:],
-            ],
-            axis=1,
-        )
-        return state * decay + held[:, 0:WIDE]
-
-    lax.fori_loop(0, nctx, scan, jnp.zeros((TILE, WIDE), F32))
-
-    for quad in range(quads // 2, quads):
-        inner(quad)
+        return state * rd[shard, 0:1, :] + ra[shard].astype(F32)
+
+    def scan_slice(quad):
+        @pl.when(my_quad == quad)
+        def _():
+            lax.fori_loop(0, nctx, scan, jnp.zeros((TILE, WIDE), F32))
 
     def y_copy(quad, way):
         if way == 0:
-            src, dst = pl.ds(2 * margin, margin), pl.ds(0, margin)
+            src, dst = pl.ds(margin, margin), pl.ds(0, margin)
         else:
-            src, dst = pl.ds(margin, margin), pl.ds(3 * margin, margin)
+            src, dst = pl.ds(0, margin), pl.ds(margin, margin)
         return pltpu.make_async_remote_copy(
-            src_ref=framed.at[quad, src],
-            dst_ref=framed.at[quad, dst],
+            src_ref=y_home.at[quad, src],
+            dst_ref=y_away.at[quad, dst],
             send_sem=ys_sems.at[quad, way],
             recv_sem=yr_sems.at[quad, way],
             device_id={"ctx": around[way]},
         )
 
-    for quad in range(quads):
-
-        def arrive(group, _, quad=quad):
+    def finish(quad):
+        def arrive(group, _):
             owner = group * quads + quad
 
             @pl.when(owner != me)
@@ -451,21 +483,54 @@
         lax.fori_loop(0, groups, arrive, 0)
         incoming = inc[quad].reshape(N, WIDE)
         fix = mm(conv_ref[0, :, N : 2 * N], incoming)
-        framed[quad, margin : margin + tok, :] = (ypart[quad] + fix * es_ref[quad]).astype(BF16)
+        y_home[quad] = (ypart[quad] + fix * es_ref[quad]).astype(BF16)
         for way in range(2):
             y_copy(quad, way).start()
 
+    for quad in range(quads):
+        with scope("pack%d" % quad):
+            pack_conv(quad + 1)
+        with scope("state%d" % quad):
+            shard_state(quad)
+        if quad == 2:
+            with scope("inner0"):
+                inner(0)
+    with scope("scan"):
+        scan_slice(0)
+        scan_slice(1)
+    with scope("inner1"):
+        inner(1)
+        inner(2)
+    with scope("scan2"):
+        scan_slice(2)
+    with scope("inner3"):
+        inner(3)
+    with scope("scan3"):
+        scan_slice(3)
+    with scope("finish0"):
+        finish(0)
+    with scope("finish1"):
+        finish(1)
+    with scope("finish2"):
+        finish(2)
+    with scope("finish3"):
+        finish(3)
+
     for i in range(blocks):
-        across = jnp.broadcast_to(dest_ref[i : i + 1, :], (SPAN, SPAN)).T - first + margin
-        for j in range(2 * blocks):
-            q_ref[i * SPAN : (i + 1) * SPAN, j * SPAN : (j + 1) * SPAN] = one_hot(
-                across == lane + j * SPAN
-            )
+        across = jnp.broadcast_to(dest_ref[i : i + 1, :], (SPAN, SPAN)).T - first
+        beside = across + jnp.where(across < 0, margin, -margin)
+        beside = jnp.where((across < 0) | (across >= tok), beside, -1)
+        for j in range(blocks):
+            at = slice(i * SPAN, (i + 1) * SPAN), slice(j * SPAN, (j + 1) * SPAN)
+            qhome_ref[at] = one_hot(across == lane + j * SPAN)
+            qaway_ref[at] = one_hot(beside == lane + j * SPAN)
+    for quad in range(quads):
+        ypart[quad] = mm(qhome_ref[...], y_home[quad])
     z_load.wait()
     for quad in range(quads):
         for way in range(2):
             y_copy(quad, way).wait_recv()
-        y_rows = mm(q_ref[...], framed[quad])
+        y_rows = ypart[quad] + mm(qaway_ref[...], y_away[quad])
         z_cols = z_ref[:, quad * WIDE : (quad + 1) * WIDE].astype(F32)
         gated = y_rows * half_silu(z_cols)
         ypart[quad] = gated
@@ -479,7 +544,8 @@
         )
         for quad in range(quads):
             at = slice(quad * WIDE, (quad + 1) * WIDE)
-            gain = gain_ref[:, at].astype(F32)
+            gain = jnp.concatenate([gain_ref[2 * quad + i : 2 * quad + i + 1, :] for i in range(2)], axis=1)
+            gain = gain.astype(F32)
             normed_ref[rows_of(i), at] = (ypart[quad, rows_of(i), :] * inv * gain).astype(BF16)
         return 0
 
@@ -549,6 +615,7 @@
         @pl.when(other != me)
         def _():
             state_copy(0, 0, other, 0).wait_send()
+            decay_copy(0, other, 0).wait_send()
             back_copy(other, 0, 0, 0).wait_send()
 
         return 0
@@ -575,6 +642,7 @@
     nhead = lax.axis_size("head")
     tok, channels = x_in.shape
     heads = dt_in.shape[1]
+    bc_width = bc_in.shape[1]
     margin = tok // 2
     blocks = tok // SPAN
     quads = channels // WIDE
@@ -587,20 +655,25 @@
     smem = pl.BlockSpec(memory_space=pltpu.SMEM)
     anywhere = pl.BlockSpec(memory_space=pl.ANY)
     scratch = [
+        pltpu.VMEM((tok, bc_width), BF16),
         pltpu.VMEM((quads, tok, WIDE), BF16),
         pltpu.VMEM((tok, channels), BF16),
         pltpu.VMEM((depth, wide), BF16),
         pltpu.VMEM((tok + TILE, tok), BF16),
         pltpu.VMEM((tok, tok), BF16),
-        pltpu.VMEM((tok, 2 * tok), BF16),
+        pltpu.VMEM((tok, tok), BF16),
+        pltpu.VMEM((tok, tok), BF16),
         pltpu.VMEM((quads + 1, tok + TILE, WIDE), BF16),
         pltpu.VMEM((quads + 1, margin + TILE, WIDE), BF16),
         pltpu.VMEM((quads + 1, margin, WIDE), BF16),
         pltpu.VMEM((2, heads, margin), BF16),
         pltpu.VMEM((2, heads, margin), BF16),
-        pltpu.VMEM((tok + TILE, WIDE), F32),
+        pltpu.VMEM((2, tok + TILE, SPAN), F32),
+        pltpu.VMEM((KCONV - 1, tok, SPAN), F32),
         pltpu.VMEM((quads + 1, tok, WIDE), BF16),
-        pltpu.VMEM((4, blocks, SPAN, SPAN), F32),
+        pltpu.VMEM((blocks, SPAN, SPAN), F32),
+        pltpu.VMEM((3, tok, 2 * SPAN), BF16),
+        pltpu.VMEM((quads, 2 * SPAN, WIDE), BF16),
         pltpu.VMEM((blocks, SPAN, SPAN), jnp.int32),
         pltpu.VMEM((blocks, 8, SPAN), F32),
         pltpu.VMEM((SPAN, SPAN), F32),
@@ -609,15 +682,19 @@
         pltpu.VMEM((quads, blocks, N, WIDE), BF16),
         pltpu.VMEM((quads, tok, WIDE), F32),
         pltpu.VMEM((quads, tok, WIDE), F32),
-        pltpu.VMEM((quads, 2 * tok, WIDE), BF16),
+        pltpu.VMEM((quads, tok, WIDE), BF16),
+        pltpu.VMEM((quads, tok, WIDE), BF16),
         pltpu.VMEM((tok, SPAN), F32),
         pltpu.VMEM((tok, channels), BF16),
-        pltpu.VMEM((quads, groups, TILE, WIDE + SPAN), BF16),
-        pltpu.VMEM((nctx, TILE, WIDE + SPAN), BF16),
+        pltpu.VMEM((quads, groups, TILE, WIDE), BF16),
+        pltpu.VMEM((nctx, TILE, WIDE), BF16),
+        pltpu.VMEM((quads, 8, WIDE), F32),
+        pltpu.VMEM((nctx, 8, WIDE), F32),
         pltpu.VMEM((nctx, TILE, WIDE), BF16),
         pltpu.VMEM((quads, groups, TILE, WIDE), BF16),
         pltpu.VMEM((nhead - 1, 2, SUBS, rows, width), BF16),
         pltpu.VMEM((nhead, 2, SUBS, rows, width), BF16),
+        dma(()),
         dma((quads,)),
         dma(()),
         dma((2, SUBS)),
@@ -629,6 +706,8 @@
         dma((nctx,)),
         dma((nctx,)),
         dma((nctx,)),
+        dma((nctx,)),
+        dma((nctx,)),
         dma((quads, 2)),
         dma((quads, 2)),
         dma((nhead - 1, 2, SUBS)),
@@ -636,11 +715,11 @@
     ]
     return pl.pallas_call(
         layer_kernel,
-        out_shape=jax.ShapeDtypeStruct((rows, wide), BF16),
+        out_shape=pltpu.VMEM((rows, wide), BF16),
         in_specs=[
             anywhere,
             anywhere,
-            vmem,
+            anywhere,
             vmem,
             vmem,
             smem,
@@ -661,7 +740,7 @@
         x_in,
         z_in,
         bc_in,
-        dt_in,
+        dt_in.T,
         destination.reshape(blocks, SPAN),
         doc_lengths,
         conv_x,
@@ -669,7 +748,7 @@
         dt_bias,
         a_log,
         skip_gain,
-        norm_gain.reshape(1, channels),
+        norm_gain.reshape(channels // SPAN, SPAN),
         out_weight,
     )
 

time: 126 us -> 113 us (0.90)
  Pallas kernels: 120 us -> 112 us
  local copies, waits for them, and re-layouts: 4.89 us -> 0.88 us
    pallas_call x1, Pallas kernels: 120 us -> 112 us  [per_device(): pl.pallas_call(layer_kernel, out_shape=pltpu.VMEM((rows, wide), BF16), in...]
    unnamed x2 -> x1, local copies, waits for them, and re-layouts: 3.61 us -> 0.88 us
    reshape x1 -> x0, local copies, waits for them, and re-layouts: 1.27 us -> none  [per_device(): norm_gain.reshape(1, channels)]
where the time goes in v3:
time: 113 us
  Pallas kernels  112 us (99%)
    pallas_call x1, Pallas kernels, per_device(): pl.pallas_call(layer_kernel, out_shape=pltpu.VMEM((rows, wide), BF16), in...  112 us

profile of v3, /device:TPU:24, one launch (start us, length us, event | category | flops | bytes accessed | tf_op | source)
XLA Modules:
  0.0 112.6 jit_solution(17531401657822413227)
XLA Ops:
  0.0 111.7 %shard_map.127 = bf16[96,4096]{1,0:T(8,128)(2,1)S(1)} custom-call(bf16[768,1024]{1,0:T(8,128)(2,1)} %x_hbm.1, bf16[768,1024]{1,0:T(8,128)(2,1)} %z_hbm.1, bf16[768,256]{1,0:T(8,128)(2,1)} %bc_hbm.1, bf16[16,768]{1,0:T(8,128)(2,1)} %bitcast.3, s32[6,128]{1,0:T(8,128)} %bitcast.4, s32[16]{0:T(128)} %lengths_ref.1, bf16[4,1024]{1,0:T(4,128)(2,1)} %convx_ref.1, ...), custom_call_target="tpu_custom_call" | custom-call | tf_op jit(solution)/shard_map/pallas_call | solution.py:716
  111.7 0.9 copy.15

commit v4 on v3

--- a/solution.py
+++ b/solution.py
@@ -45,17 +45,22 @@
     x_hbm,
     z_hbm,
     bc_hbm,
-    dt_ref,
-    dest_ref,
+    dt_hbm,
+    dest_hbm,
     lengths_ref,
-    convx_ref,
-    convbc_ref,
+    convx_hbm,
+    convbc_hbm,
     bias_ref,
     alog_ref,
     skip_ref,
-    gain_ref,
+    gain_hbm,
     w_hbm,
     out_ref,
+    dt_ref,
+    dest_ref,
+    convx_ref,
+    convbc_ref,
+    gain_ref,
     bc_ref,
     x_ref,
     z_ref,
@@ -95,19 +100,20 @@
     inc,
     sbuf,
     rbuf,
+    small_sems,
     bc_sem,
     x_sems,
     z_sem,
-    w_sems,
+    w_sem,
     xs_sems,
     xr_sems,
     ds_sems,
     dr_sems,
-    as_sems,
-    ar_sems,
-    ads_sems,
-    adr_sems,
-    rs_sems,
+    as_sem,
+    ar_sem,
+    ads_sem,
+    adr_sem,
+    rs_sem,
     rr_sems,
     ys_sems,
     yr_sems,
@@ -135,27 +141,51 @@
         pl.semaphore_signal(barrier, inc=1, device_id={"ctx": lax.rem(me + j, nctx)})
         return 0
 
-    lax.fori_loop(1, nctx, greet, 0)
+    lax.fori_loop(1, nctx, greet, 0, unroll=True)
     for hop in hops:
         pl.semaphore_signal(barrier, inc=1, device_id={"head": hop})
 
+    may_send = (me != nctx - 1, me != 0)
+    may_get = (me != 0, me != nctx - 1)
+
+    def wait_for(ref, sem):
+        pltpu.make_async_copy(ref, ref, sem).wait()
+
+    small_loads = [
+        pltpu.make_async_copy(src, dst, small_sems.at[i])
+        for i, (src, dst) in enumerate(
+            (
+                (dest_hbm, dest_ref),
+                (dt_hbm, dt_ref),
+                (convx_hbm, convx_ref),
+                (convbc_hbm, convbc_ref),
+                (gain_hbm, gain_ref),
+            )
+        )
+    ]
     bc_load = pltpu.make_async_copy(bc_hbm, bc_ref, bc_sem)
+    small_loads[0].start()
     bc_load.start()
+    for load in small_loads[1:]:
+        load.start()
+
     x_loads = [
         pltpu.make_async_copy(x_hbm.at[:, pl.ds(c * WIDE, WIDE)], x_ref.at[c], x_sems.at[c])
         for c in range(quads)
     ]
     z_load = pltpu.make_async_copy(z_hbm, z_ref, z_sem)
     wide = w_ref.shape[1]
+    rows = out_ref.shape[0]
     width = wide // (2 * SUBS)
     w_loads = []
     for sub in range(SUBS):
         for way in range(2):
             w_cols = pl.ds((way * SUBS + sub) * width, width)
             w_loads.append(
-                pltpu.make_async_copy(w_hbm.at[:, w_cols], w_ref.at[:, w_cols], w_sems.at[way, sub])
+                pltpu.make_async_copy(w_hbm.at[:, w_cols], w_ref.at[:, w_cols], w_sem)
             )
 
+    small_loads[0].wait()
     rel_row = jnp.concatenate([dest_ref[i : i + 1, :] for i in range(blocks)], axis=1) - first
     slot = iota((margin + TILE, tok), 0)
     goal = jnp.where(slot < margin, slot + tok, slot + (tok - TILE - margin))
@@ -170,7 +200,7 @@
         return pltpu.make_async_remote_copy(
             src_ref=src,
             dst_ref=dst,
-            send_sem=xs_sems.at[chunk, way],
+            send_sem=xs_sems.at[way],
             recv_sem=xr_sems.at[chunk, way],
             device_id={"ctx": around[way]},
         )
@@ -187,6 +217,8 @@
     def source(chunk):
         return bc_ref[...] if chunk == 0 else x_ref[chunk - 1]
 
+    for load in small_loads[1:]:
+        load.wait()
     dt_rows = dt_ref[...]
     dts[0] = nt(dt_rows, pout_ref[0:margin, :]).astype(BF16)
     dts[1] = nt(dt_rows, pout_ref[margin + TILE :, :]).astype(BF16)
@@ -197,20 +229,41 @@
 
     pl.semaphore_wait(barrier, nctx + 1)
     for way in range(2):
-        dt_copy(way).start()
-    for way in range(2):
-        exchange(0, way).start()
-    for chunk in range(1, quads + 1):
+
+        @pl.when(may_send[way])
+        def _():
+            dt_copy(way).start()
+            exchange(0, way).start()
+
+
+    def send_out(chunk):
         x_loads[chunk - 1].wait()
         snd[chunk] = mm(pout_ref[...], source(chunk)).astype(BF16)
         for way in range(2):
-            exchange(chunk, way).start()
+
+            @pl.when(may_send[way])
+            def _():
+                exchange(chunk, way).start()
+
+
+    send_out(1)
+    send_out(2)
 
     z_load.start()
     for load in w_loads:
         load.start()
 
     home_ref[...] = one_hot(iota((tok, tok), 0) == rel_row)
+    for way in range(2):
+
+        @pl.when(jnp.logical_not(may_get[way]))
+        def _():
+            landing = (rcvp, rcvn)[way]
+            landing[...] = jnp.zeros_like(landing)
+            dtr[way] = jnp.zeros_like(dtr[way])
+            at = pl.ds(way * margin, margin)
+            y_away[:, at, :] = jnp.zeros((quads, margin, WIDE), BF16)
+
 
     row16 = iota((heads, SPAN), 0)
     bias = jnp.zeros((heads, SPAN), F32)
@@ -220,7 +273,11 @@
         alog = jnp.where(row16 == h, alog_ref[h], alog)
     neg_rate = -jnp.exp(alog)
     for way in range(2):
-        dt_copy(way).wait_recv()
+
+        @pl.when(may_get[way])
+        def _():
+            dt_copy(way).wait_recv()
+
     dt_home = nt(dt_rows, home_ref[...])
     home_first = mm(home_ref[...], source(0))
     dt_raw = dt_home + jnp.concatenate([dtr[0].astype(F32), dtr[1].astype(F32)], axis=1)
@@ -302,7 +359,11 @@
         if home is None:
             home = mm(home_ref[...], source(chunk))
         for way in range(2):
-            exchange(chunk, way).wait_recv()
+
+            @pl.when(may_get[way])
+            def _():
+                exchange(chunk, way).wait_recv()
+
         if chunk == 0:
             taps = convbc_ref[...].astype(F32)
         else:
@@ -349,21 +410,21 @@
 
     lax.fori_loop(0, blocks, prepare, 0, unroll=True)
 
-    def state_copy(quad, group, owner, source_id):
+    def state_copy(quad, group, owner):
         return pltpu.make_async_remote_copy(
             src_ref=sa.at[quad, group],
-            dst_ref=ra.at[source_id],
-            send_sem=as_sems.at[owner],
-            recv_sem=ar_sems.at[source_id],
+            dst_ref=ra.at[lax.rem(me + nctx - owner, nctx)],
+            send_sem=as_sem,
+            recv_sem=ar_sem,
             device_id={"ctx": owner},
         )
 
-    def decay_copy(quad, owner, source_id):
+    def decay_copy(quad, owner):
         return pltpu.make_async_remote_copy(
             src_ref=da.at[quad, pl.ds(0, 1)],
-            dst_ref=rd.at[source_id, pl.ds(0, 1)],
-            send_sem=ads_sems.at[owner],
-            recv_sem=adr_sems.at[source_id],
+            dst_ref=rd.at[lax.rem(me + nctx - owner, nctx), pl.ds(0, 1)],
+            send_sem=ads_sem,
+            recv_sem=adr_sem,
             device_id={"ctx": owner},
         )
 
@@ -386,13 +447,13 @@
 
             @pl.when(owner != me)
             def _():
-                state_copy(quad, group, owner, me).start()
-                decay_copy(quad, owner, me).start()
+                state_copy(quad, group, owner).start()
+                decay_copy(quad, owner).start()
 
             @pl.when(owner == me)
             def _():
-                ra[me] = sa[quad, group]
-                rd[me] = da[quad]
+                ra[0] = sa[quad, group]
+                rd[0] = da[quad]
 
             return 0
 
@@ -428,12 +489,12 @@
     my_quad = lax.rem(me, quads)
     my_group = lax.div(me, quads)
 
-    def back_copy(shard, quad, group, owner):
+    def back_copy(shard, quad, group):
         return pltpu.make_async_remote_copy(
             src_ref=ret.at[shard],
             dst_ref=inc.at[quad, group],
-            send_sem=rs_sems.at[shard],
-            recv_sem=rr_sems.at[owner],
+            send_sem=rs_sem,
+            recv_sem=rr_sems.at[quad],
             device_id={"ctx": shard},
         )
 
@@ -442,19 +503,20 @@
 
         @pl.when(shard != me)
         def _():
-            back_copy(shard, my_quad, my_group, me).start()
-            state_copy(0, 0, 0, shard).wait_recv()
-            decay_copy(0, 0, shard).wait_recv()
+            back_copy(shard, my_quad, my_group).start()
 
         @pl.when(shard == me)
         def _():
             inc[my_quad, my_group] = state.astype(BF16)
 
-        return state * rd[shard, 0:1, :] + ra[shard].astype(F32)
+        place = lax.rem(shard + nctx - me, nctx)
+        return state * rd[place, 0:1, :] + ra[place].astype(F32)
 
     def scan_slice(quad):
         @pl.when(my_quad == quad)
         def _():
+            wait_for(ra.at[pl.ds(1, nctx - 1)], ar_sem)
+            wait_for(rd.at[pl.ds(1, nctx - 1), pl.ds(0, 1)], adr_sem)
             lax.fori_loop(0, nctx, scan, jnp.zeros((TILE, WIDE), F32))
 
     def y_copy(quad, way):
@@ -465,50 +527,61 @@
         return pltpu.make_async_remote_copy(
             src_ref=y_home.at[quad, src],
             dst_ref=y_away.at[quad, dst],
-            send_sem=ys_sems.at[quad, way],
+            send_sem=ys_sems.at[way],
             recv_sem=yr_sems.at[quad, way],
             device_id={"ctx": around[way]},
         )
 
     def finish(quad):
-        def arrive(group, _):
-            owner = group * quads + quad
-
-            @pl.when(owner != me)
-            def _():
-                back_copy(0, quad, group, owner).wait_recv()
-
-            return 0
-
-        lax.fori_loop(0, groups, arrive, 0)
+        @pl.when(my_quad != quad)
+        def _():
+            wait_for(inc.at[quad], rr_sems.at[quad])
+
+        @pl.when(my_quad == quad)
+        def _():
+            wait_for(inc.at[quad, pl.ds(1, groups - 1)], rr_sems.at[quad])
+
         incoming = inc[quad].reshape(N, WIDE)
         fix = mm(conv_ref[0, :, N : 2 * N], incoming)
         y_home[quad] = (ypart[quad] + fix * es_ref[quad]).astype(BF16)
         for way in range(2):
-            y_copy(quad, way).start()
-
-    for quad in range(quads):
+
+            @pl.when(may_send[way])
+            def _():
+                y_copy(quad, way).start()
+
+
+    def work(quad):
         with scope("pack%d" % quad):
             pack_conv(quad + 1)
         with scope("state%d" % quad):
             shard_state(quad)
-        if quad == 2:
-            with scope("inner0"):
-                inner(0)
-    with scope("scan"):
+
+    with scope("out3"):
+        send_out(3)
+    work(0)
+    with scope("out4"):
+        send_out(4)
+    work(1)
+    with scope("inner0"):
+        inner(0)
+    work(2)
+    with scope("scan0"):
         scan_slice(0)
+    work(3)
+    with scope("scan1"):
         scan_slice(1)
     with scope("inner1"):
         inner(1)
-        inner(2)
     with scope("scan2"):
         scan_slice(2)
-    with scope("inner3"):
+    with scope("finish0"):
+        finish(0)
+    with scope("inner2"):
+        inner(2)
         inner(3)
     with scope("scan3"):
         scan_slice(3)
-    with scope("finish0"):
-        finish(0)
     with scope("finish1"):
         finish(1)
     with scope("finish2"):
@@ -527,51 +600,69 @@
     for quad in range(quads):
         ypart[quad] = mm(qhome_ref[...], y_home[quad])
     z_load.wait()
+    rbuf[0] = jnp.zeros_like(rbuf[0])
+    wait_for(w_ref, w_sem)
+
+    def gate(quad, at, z_at):
+        y_rows = ypart[quad, at, :] + mm(qaway_ref[at, :], y_away[quad])
+        gated = y_rows * half_silu(z_ref[at, z_at].astype(F32))
+        square = gated * gated
+        return gated, square[:, 0:SPAN] + square[:, SPAN:]
+
     for quad in range(quads):
         for way in range(2):
-            y_copy(quad, way).wait_recv()
-        y_rows = ypart[quad] + mm(qaway_ref[...], y_away[quad])
-        z_cols = z_ref[:, quad * WIDE : (quad + 1) * WIDE].astype(F32)
-        gated = y_rows * half_silu(z_cols)
-        ypart[quad] = gated
-        square = gated * gated
-        square = square[:, 0:SPAN] + square[:, SPAN:]
-        ss_ref[...] = square if quad == 0 else ss_ref[...] + square
-
-    def norm(i, _):
-        inv = lax.rsqrt(
-            jnp.sum(ss_ref[rows_of(i), :], axis=1, keepdims=True) * (1.0 / (quads * WIDE)) + 1e-05
-        )
+
+            @pl.when(may_get[way])
+            def _():
+                y_copy(quad, way).wait_recv()
+
+        if quad < quads - 1:
+            gated, square = gate(quad, pl.ds(0, tok), pl.ds(quad * WIDE, WIDE))
+            ypart[quad] = gated
+            ss_ref[...] = square if quad == 0 else ss_ref[...] + square
+
+    def ready(chunk):
+        at = pl.ds(pl.multiple_of(chunk * rows, rows), rows)
+        gated, square = gate(quads - 1, at, pl.ds((quads - 1) * WIDE, WIDE))
+        total = jnp.sum(ss_ref[at, :] + square, axis=1, keepdims=True)
+        inv = lax.rsqrt(total * (1.0 / (quads * WIDE)) + 1e-05)
         for quad in range(quads):
-            at = slice(quad * WIDE, (quad + 1) * WIDE)
             gain = jnp.concatenate([gain_ref[2 * quad + i : 2 * quad + i + 1, :] for i in range(2)], axis=1)
-            gain = gain.astype(F32)
-            normed_ref[rows_of(i), at] = (ypart[quad, rows_of(i), :] * inv * gain).astype(BF16)
-        return 0
-
-    lax.fori_loop(0, blocks, norm, 0)
-
-    rows = out_ref.shape[0]
-    rbuf[0] = jnp.zeros_like(rbuf[0])
-    for load in w_loads:
-        load.wait()
+            value = gated if quad == quads - 1 else ypart[quad, at, :]
+            normed_ref[at, quad * WIDE : (quad + 1) * WIDE] = (
+                value * inv * gain.astype(F32)
+            ).astype(BF16)
 
     def ring(step, way, sub):
         return pltpu.make_async_remote_copy(
             src_ref=sbuf.at[step, way, sub],
             dst_ref=rbuf.at[step + 1, way, sub],
-            send_sem=send_sems.at[step, way, sub],
+            send_sem=send_sems.at[way, sub],
             recv_sem=recv_sems.at[step, way, sub],
             device_id={"head": hops[way]},
         )
 
+    def chunk_of(step, way):
+        back = lax.rem(mz + 2 * nhead - 1 - step, nhead)
+        return jnp.where(way == 0, back, lax.rem(mz + 1 + step, nhead))
+
     def one(step, _):
+        def ready_way(way, _):
+            @pl.when((step < nhead // 2) & ((step < nhead // 2 - 1) | (way == 0)))
+            def _():
+                ready(chunk_of(step, way))
+
+            return 0
+
+        lax.fori_loop(0, 2, ready_way, 0)
+
+        @pl.when(step == nhead // 2)
+        def _():
+            ready(mz)
+
         for sub in range(SUBS):
             for way in range(2):
-                if way == 0:
-                    chunk = lax.rem(mz + 2 * nhead - 1 - step, nhead)
-                else:
-                    chunk = lax.rem(mz + 1 + step, nhead)
+                chunk = chunk_of(step, way)
                 at = (way * SUBS + sub) * width
                 part = mm(
                     normed_ref[pl.ds(pl.multiple_of(chunk * rows, rows), rows), :],
@@ -581,6 +672,7 @@
                 @pl.when(step > 0)
                 def _():
                     ring(step - 1, way, sub).wait_recv()
+                    ring(step - 1, way, sub).wait_send()
 
                 total = (part + rbuf[step, way, sub].astype(F32)).astype(BF16)
 
@@ -595,32 +687,21 @@
 
         return 0
 
-    lax.fori_loop(0, nhead, one, 0)
-
-    def drain(step, _):
-        for sub in range(SUBS):
-            for way in range(2):
-                ring(step, way, sub).wait_send()
-        return 0
-
-    lax.fori_loop(0, nhead - 1, drain, 0)
+    lax.fori_loop(0, nhead - 1, one, 0)
+
     for way in range(2):
-        dt_copy(way).wait_send()
-        for chunk in range(quads + 1):
-            exchange(chunk, way).wait_send()
-        for quad in range(quads):
-            y_copy(quad, way).wait_send()
-
-    def drain_states(other, _):
-        @pl.when(other != me)
-        def _():
-            state_copy(0, 0, other, 0).wait_send()
-            decay_copy(0, other, 0).wait_send()
-            back_copy(other, 0, 0, 0).wait_send()
-
-        return 0
-
-    lax.fori_loop(0, nctx, drain_states, 0)
+
+        @pl.when(may_send[way])
+        def _():
+            dt_copy(way).wait_send()
+            sent = (pl.ds(0, margin + TILE), pl.ds(margin + TILE, margin))[way]
+            wait_for(snd.at[:, sent], xs_sems.at[way])
+            wait_for(y_home.at[:, pl.ds(0, margin)], ys_sems.at[way])
+
+    wait_for(ra.at[pl.ds(1, nctx - 1)], as_sem)
+    wait_for(rd.at[pl.ds(1, nctx - 1), pl.ds(0, 1)], ads_sem)
+    wait_for(ret.at[pl.ds(1, nctx - 1)], rs_sem)
+    lax.fori_loop(nhead - 1, nhead, one, 0)
 
 
 def per_device(
@@ -655,6 +736,11 @@
     smem = pl.BlockSpec(memory_space=pltpu.SMEM)
     anywhere = pl.BlockSpec(memory_space=pl.ANY)
     scratch = [
+        pltpu.VMEM((heads, tok), BF16),
+        pltpu.VMEM((blocks, SPAN), jnp.int32),
+        pltpu.VMEM(conv_x.shape, BF16),
+        pltpu.VMEM(conv_bc.shape, BF16),
+        pltpu.VMEM((channels // SPAN, SPAN), BF16),
         pltpu.VMEM((tok, bc_width), BF16),
         pltpu.VMEM((quads, tok, WIDE), BF16),
         pltpu.VMEM((tok, channels), BF16),
@@ -694,23 +780,24 @@
         pltpu.VMEM((quads, groups, TILE, WIDE), BF16),
         pltpu.VMEM((nhead - 1, 2, SUBS, rows, width), BF16),
         pltpu.VMEM((nhead, 2, SUBS, rows, width), BF16),
+        dma((5,)),
         dma(()),
         dma((quads,)),
         dma(()),
-        dma((2, SUBS)),
-        dma((quads + 1, 2)),
+        dma(()),
+        dma((2,)),
         dma((quads + 1, 2)),
         dma((2,)),
         dma((2,)),
-        dma((nctx,)),
-        dma((nctx,)),
-        dma((nctx,)),
-        dma((nctx,)),
-        dma((nctx,)),
-        dma((nctx,)),
+        dma(()),
+        dma(()),
+        dma(()),
+        dma(()),
+        dma(()),
+        dma((quads,)),
+        dma((2,)),
         dma((quads, 2)),
-        dma((quads, 2)),
-        dma((nhead - 1, 2, SUBS)),
+        dma((2, SUBS)),
         dma((nhead - 1, 2, SUBS)),
     ]
     return pl.pallas_call(
@@ -720,15 +807,15 @@
             anywhere,
             anywhere,
             anywhere,
-            vmem,
-            vmem,
+            anywhere,
+            anywhere,
             smem,
-            vmem,
-            vmem,
+            anywhere,
+            anywhere,
             smem,
             smem,
             smem,
-            vmem,
+            anywhere,
             anywhere,
         ],
         out_specs=vmem,

time: 113 us -> 108 us (0.956)
  Pallas kernels: 112 us -> 107 us
    pallas_call x1, Pallas kernels: 112 us -> 107 us  [per_device(): pl.pallas_call(layer_kernel, out_shape=pltpu.VMEM((rows, wide), BF16), in...]
where the time goes in v4:
time: 108 us
  Pallas kernels  107 us (99%)
    pallas_call x1, Pallas kernels, per_device(): pl.pallas_call(layer_kernel, out_shape=pltpu.VMEM((rows, wide), BF16), in...  107 us

profile of v4, /device:TPU:24, one launch (start us, length us, event | category | flops | bytes accessed | tf_op | source)
XLA Modules:
  0.0 107.9 jit_solution(8377465461334631777)
XLA Ops:
  0.0 107.0 %shard_map.127 = bf16[96,4096]{1,0:T(8,128)(2,1)S(1)} custom-call(bf16[768,1024]{1,0:T(8,128)(2,1)} %x_hbm.1, bf16[768,1024]{1,0:T(8,128)(2,1)} %z_hbm.1, bf16[768,256]{1,0:T(8,128)(2,1)} %bc_hbm.1, bf16[16,768]{1,0:T(8,128)(2,1)} %bitcast.3, s32[6,128]{1,0:T(8,128)} %bitcast.4, s32[16]{0:T(128)} %lengths_ref.1, bf16[4,1024]{1,0:T(4,128)(2,1)} %convx_hbm.1, ...), custom_call_target="tpu_custom_call" | custom-call | tf_op jit(solution)/shard_map/pallas_call | solution.py:803
  107.0 0.9 copy.15

commit v5 on v4

--- a/solution.py
+++ b/solution.py
@@ -47,15 +47,19 @@
     bc_hbm,
     dt_hbm,
     dest_hbm,
-    lengths_ref,
+    lengths_hbm,
     convx_hbm,
     convbc_hbm,
+    bias_hbm,
+    alog_hbm,
+    skip_hbm,
+    gain_hbm,
+    w_hbm,
+    out_ref,
+    lengths_ref,
     bias_ref,
     alog_ref,
     skip_ref,
-    gain_hbm,
-    w_hbm,
-    out_ref,
     dt_ref,
     dest_ref,
     convx_ref,
@@ -77,6 +81,7 @@
     xext,
     mask_ref,
     conv_ref,
+    later_ref,
     cols_ref,
     part_ref,
     head_ref,
@@ -135,16 +140,6 @@
     around = (lax.rem(me + 1, nctx), lax.rem(me + nctx - 1, nctx))
     hops = (lax.rem(mz + 1, nhead), lax.rem(mz + nhead - 1, nhead))
 
-    barrier = pltpu.get_barrier_semaphore()
-
-    def greet(j, _):
-        pl.semaphore_signal(barrier, inc=1, device_id={"ctx": lax.rem(me + j, nctx)})
-        return 0
-
-    lax.fori_loop(1, nctx, greet, 0, unroll=True)
-    for hop in hops:
-        pl.semaphore_signal(barrier, inc=1, device_id={"head": hop})
-
     may_send = (me != nctx - 1, me != 0)
     may_get = (me != 0, me != nctx - 1)
 
@@ -160,12 +155,25 @@
                 (convx_hbm, convx_ref),
                 (convbc_hbm, convbc_ref),
                 (gain_hbm, gain_ref),
+                (lengths_hbm, lengths_ref),
+                (bias_hbm, bias_ref),
+                (alog_hbm, alog_ref),
+                (skip_hbm, skip_ref),
             )
         )
     ]
     bc_load = pltpu.make_async_copy(bc_hbm, bc_ref, bc_sem)
     small_loads[0].start()
     bc_load.start()
+    barrier = pltpu.get_barrier_semaphore()
+
+    def greet(j, _):
+        pl.semaphore_signal(barrier, inc=1, device_id={"ctx": lax.rem(me + j, nctx)})
+        return 0
+
+    lax.fori_loop(1, nctx, greet, 0, unroll=True)
+    for hop in hops:
+        pl.semaphore_signal(barrier, inc=1, device_id={"head": hop})
     for load in small_loads[1:]:
         load.start()
 
@@ -217,8 +225,7 @@
     def source(chunk):
         return bc_ref[...] if chunk == 0 else x_ref[chunk - 1]
 
-    for load in small_loads[1:]:
-        load.wait()
+    small_loads[1].wait()
     dt_rows = dt_ref[...]
     dts[0] = nt(dt_rows, pout_ref[0:margin, :]).astype(BF16)
     dts[1] = nt(dt_rows, pout_ref[margin + TILE :, :]).astype(BF16)
@@ -236,9 +243,10 @@
             exchange(0, way).start()
 
 
-    def send_out(chunk):
-        x_loads[chunk - 1].wait()
+    def make_out(chunk):
         snd[chunk] = mm(pout_ref[...], source(chunk)).astype(BF16)
+
+    def start_out(chunk):
         for way in range(2):
 
             @pl.when(may_send[way])
@@ -246,8 +254,10 @@
                 exchange(chunk, way).start()
 
 
-    send_out(1)
-    send_out(2)
+    for chunk in (1, 2):
+        x_loads[chunk - 1].wait()
+        make_out(chunk)
+        start_out(chunk)
 
     z_load.start()
     for load in w_loads:
@@ -265,6 +275,13 @@
             y_away[:, at, :] = jnp.zeros((quads, margin, WIDE), BF16)
 
 
+    for load in x_loads[2:]:
+        load.wait()
+    make_out(3)
+    start_out(3)
+
+    for load in small_loads[2:]:
+        load.wait()
     row16 = iota((heads, SPAN), 0)
     bias = jnp.zeros((heads, SPAN), F32)
     alog = jnp.zeros((heads, SPAN), F32)
@@ -326,17 +343,31 @@
     carried = jnp.where(last_start < block_start[0:1, :], jnp.exp(last), 0.0)
     shard_decay = jnp.where(last_start < first, jnp.exp(last + offset), 0.0)
     carried = jnp.broadcast_to(carried, (8, SPAN))
+    later_ref[0] = LOG2E * cum
+    later_ref[1] = entry
+    later_ref[2] = entry_shard
+
+    def turned(array, b):
+        turn = (SPAN - b * heads) % SPAN
+        return pltpu.roll(array, turn, 1) if turn else array
+
+    def split(kind, b, array):
+        array = turned(array, b)
+        rough = array.astype(BF16)
+        fine = (array - rough.astype(F32)).astype(BF16)
+        part_ref[kind, b * SPAN : (b + 1) * SPAN, 0:SPAN] = rough
+        part_ref[kind, b * SPAN : (b + 1) * SPAN, SPAN:] = fine
+
+    def later():
+        for b in range(blocks):
+            cols_ref[b] = turned(later_ref[0], b)
+            split(1, b, later_ref[1])
+            split(2, b, later_ref[2])
+
     for b in range(blocks):
-        turn = (SPAN - b * heads) % SPAN
-        cols_ref[b] = pltpu.roll(LOG2E * cum, turn, 1) if turn else LOG2E * cum
-        for kind, array in enumerate((w_cols, entry, entry_shard)):
-            array = pltpu.roll(array, turn, 1) if turn else array
-            rough = array.astype(BF16)
-            fine = (array - rough.astype(F32)).astype(BF16)
-            part_ref[kind, b * SPAN : (b + 1) * SPAN, 0:SPAN] = rough
-            part_ref[kind, b * SPAN : (b + 1) * SPAN, SPAN:] = fine
-        ds_ref[b] = pltpu.roll(doc_start, turn, 1) if turn else doc_start
-        car_ref[b] = pltpu.roll(carried, turn, 1) if turn else carried
+        split(0, b, w_cols)
+        ds_ref[b] = turned(doc_start, b)
+        car_ref[b] = turned(carried, b)
     for quad in range(quads):
         key = iota((2 * SPAN, WIDE), 0) & (SPAN - 1)
         head = lax.shift_right_logical(iota((2 * SPAN, WIDE), 1), 6) + 4 * quad
@@ -355,15 +386,17 @@
     def rows_of(b):
         return pl.ds(pl.multiple_of(b * SPAN, SPAN), SPAN)
 
-    def pack_conv(chunk, home=None):
-        if home is None:
-            home = mm(home_ref[...], source(chunk))
+    def pack_conv(chunk, home):
         for way in range(2):
 
             @pl.when(may_get[way])
             def _():
                 exchange(chunk, way).wait_recv()
 
+        if chunk == 0:
+            make_out(quads)
+        if chunk < quads:
+            ypart[chunk] = mm(home_ref[...], source(chunk + 1))
         if chunk == 0:
             taps = convbc_ref[...].astype(F32)
         else:
@@ -377,18 +410,17 @@
                 chunk, 0:margin, at
             ].astype(F32)
             xext[half, TILE + margin :, :] = home[margin:, at] + rcvn[chunk, :, at].astype(F32)
-        with scope("conv"):
-            for half in range(2):
-                at = slice(half * SPAN, (half + 1) * SPAN)
-                for b in range(blocks):
-                    base = b * SPAN + TILE
-                    total = taps[3:4, at] * xext[half, base : base + SPAN, :]
-                    for tap in range(KCONV - 1):
-                        back = KCONV - 1 - tap
-                        piece = xext[half, base - back : base - back + SPAN, :]
-                        usable = mask_ref[tap, b * SPAN : (b + 1) * SPAN, :]
-                        total = total + taps[tap : tap + 1, at] * (usable * piece)
-                    conv_ref[chunk, b * SPAN : (b + 1) * SPAN, at] = half_silu(total).astype(BF16)
+        for half in range(2):
+            at = slice(half * SPAN, (half + 1) * SPAN)
+            for b in range(blocks):
+                base = b * SPAN + TILE
+                total = taps[3:4, at] * xext[half, base : base + SPAN, :]
+                for tap in range(KCONV - 1):
+                    back = KCONV - 1 - tap
+                    piece = xext[half, base - back : base - back + SPAN, :]
+                    usable = mask_ref[tap, b * SPAN : (b + 1) * SPAN, :]
+                    total = total + taps[tap : tap + 1, at] * (usable * piece)
+                conv_ref[chunk, b * SPAN : (b + 1) * SPAN, at] = half_silu(total).astype(BF16)
 
     for b in range(blocks):
         begins = jnp.broadcast_to(ds_ref[b][:, 0:1], (SPAN, SPAN)) - (first + b * SPAN) - row
@@ -552,18 +584,15 @@
 
 
     def work(quad):
-        with scope("pack%d" % quad):
-            pack_conv(quad + 1)
-        with scope("state%d" % quad):
+        with scope("work%d" % quad):
+            pack_conv(quad + 1, ypart[quad])
             shard_state(quad)
 
-    with scope("out3"):
-        send_out(3)
     work(0)
-    with scope("out4"):
-        send_out(4)
+    start_out(quads)
     work(1)
     with scope("inner0"):
+        later()
         inner(0)
     work(2)
     with scope("scan0"):
@@ -586,9 +615,6 @@
         finish(1)
     with scope("finish2"):
         finish(2)
-    with scope("finish3"):
-        finish(3)
-
     for i in range(blocks):
         across = jnp.broadcast_to(dest_ref[i : i + 1, :], (SPAN, SPAN)).T - first
         beside = across + jnp.where(across < 0, margin, -margin)
@@ -597,11 +623,12 @@
             at = slice(i * SPAN, (i + 1) * SPAN), slice(j * SPAN, (j + 1) * SPAN)
             qhome_ref[at] = one_hot(across == lane + j * SPAN)
             qaway_ref[at] = one_hot(beside == lane + j * SPAN)
-    for quad in range(quads):
-        ypart[quad] = mm(qhome_ref[...], y_home[quad])
     z_load.wait()
     rbuf[0] = jnp.zeros_like(rbuf[0])
     wait_for(w_ref, w_sem)
+
+    def gather_home(quad):
+        ypart[quad] = mm(qhome_ref[...], y_home[quad])
 
     def gate(quad, at, z_at):
         y_rows = ypart[quad, at, :] + mm(qaway_ref[at, :], y_away[quad])
@@ -609,17 +636,29 @@
         square = gated * gated
         return gated, square[:, 0:SPAN] + square[:, SPAN:]
 
-    for quad in range(quads):
+    def gather(quad):
         for way in range(2):
 
             @pl.when(may_get[way])
             def _():
                 y_copy(quad, way).wait_recv()
 
+        if quad == 1:
+            gather_home(quads - 1)
         if quad < quads - 1:
             gated, square = gate(quad, pl.ds(0, tok), pl.ds(quad * WIDE, WIDE))
             ypart[quad] = gated
             ss_ref[...] = square if quad == 0 else ss_ref[...] + square
+
+    for quad in range(quads - 1):
+        gather_home(quad)
+    with scope("gather0"):
+        gather(0)
+    with scope("finish3"):
+        finish(3)
+    for quad in range(1, quads):
+        with scope("gather%d" % quad):
+            gather(quad)
 
     def ready(chunk):
         at = pl.ds(pl.multiple_of(chunk * rows, rows), rows)
@@ -733,9 +772,12 @@
     width = wide // (2 * SUBS)
     dma = pltpu.SemaphoreType.DMA
     vmem = pl.BlockSpec(memory_space=pltpu.VMEM)
-    smem = pl.BlockSpec(memory_space=pltpu.SMEM)
     anywhere = pl.BlockSpec(memory_space=pl.ANY)
     scratch = [
+        pltpu.SMEM(doc_lengths.shape, jnp.int32),
+        pltpu.SMEM((heads,), F32),
+        pltpu.SMEM((heads,), F32),
+        pltpu.SMEM((heads,), F32),
         pltpu.VMEM((heads, tok), BF16),
         pltpu.VMEM((blocks, SPAN), jnp.int32),
         pltpu.VMEM(conv_x.shape, BF16),
@@ -757,6 +799,7 @@
         pltpu.VMEM((2, tok + TILE, SPAN), F32),
         pltpu.VMEM((KCONV - 1, tok, SPAN), F32),
         pltpu.VMEM((quads + 1, tok, WIDE), BF16),
+        pltpu.VMEM((3, SPAN, SPAN), F32),
         pltpu.VMEM((blocks, SPAN, SPAN), F32),
         pltpu.VMEM((3, tok, 2 * SPAN), BF16),
         pltpu.VMEM((quads, 2 * SPAN, WIDE), BF16),
@@ -780,7 +823,7 @@
         pltpu.VMEM((quads, groups, TILE, WIDE), BF16),
         pltpu.VMEM((nhead - 1, 2, SUBS, rows, width), BF16),
         pltpu.VMEM((nhead, 2, SUBS, rows, width), BF16),
-        dma((5,)),
+        dma((9,)),
         dma(()),
         dma((quads,)),
         dma(()),
@@ -809,12 +852,12 @@
             anywhere,
             anywhere,
             anywhere,
-            smem,
-            anywhere,
-            anywhere,
-            smem,
-            smem,
-            smem,
+            anywhere,
+            anywhere,
+            anywhere,
+            anywhere,
+            anywhere,
+            anywhere,
             anywhere,
             anywhere,
         ],

time: 108 us -> 107 us (level)
    pallas_call x1, Pallas kernels: 107 us -> 106 us  [per_device(): pl.pallas_call(layer_kernel, out_shape=pltpu.VMEM((rows, wide), BF16), in...]
where the time goes in v5:
time: 107 us
  Pallas kernels  106 us (99%)
    pallas_call x1, Pallas kernels, per_device(): pl.pallas_call(layer_kernel, out_shape=pltpu.VMEM((rows, wide), BF16), in...  106 us

profile of v5, /device:TPU:24, one launch (start us, length us, event | category | flops | bytes accessed | tf_op | source)
XLA Modules:
  0.0 106.7 jit_solution(671699173583757563)
XLA Ops:
  0.0 105.8 %shard_map.127 = bf16[96,4096]{1,0:T(8,128)(2,1)S(1)} custom-call(bf16[768,1024]{1,0:T(8,128)(2,1)} %x_hbm.1, bf16[768,1024]{1,0:T(8,128)(2,1)} %z_hbm.1, bf16[768,256]{1,0:T(8,128)(2,1)} %bc_hbm.1, bf16[16,768]{1,0:T(8,128)(2,1)} %bitcast.3, s32[6,128]{1,0:T(8,128)} %bitcast.4, s32[16]{0:T(128)} %lengths_hbm.1, bf16[4,1024]{1,0:T(4,128)(2,1)} %convx_hbm.1, ...), custom_call_target="tpu_custom_call" | custom-call | tf_op jit(solution)/shard_map/pallas_call | solution.py:846
  105.8 0.9 copy.15

commit v6 on v5

--- a/solution.py
+++ b/solution.py
@@ -608,13 +608,14 @@
         finish(0)
     with scope("inner2"):
         inner(2)
-        inner(3)
     with scope("scan3"):
         scan_slice(3)
     with scope("finish1"):
         finish(1)
     with scope("finish2"):
         finish(2)
+    with scope("inner3"):
+        inner(3)
     for i in range(blocks):
         across = jnp.broadcast_to(dest_ref[i : i + 1, :], (SPAN, SPAN)).T - first
         beside = across + jnp.where(across < 0, margin, -margin)
@@ -643,33 +644,33 @@
             def _():
                 y_copy(quad, way).wait_recv()
 
-        if quad == 1:
-            gather_home(quads - 1)
+        if quad < quads - 1:
+            gather_home(quad + 1)
         if quad < quads - 1:
             gated, square = gate(quad, pl.ds(0, tok), pl.ds(quad * WIDE, WIDE))
             ypart[quad] = gated
             ss_ref[...] = square if quad == 0 else ss_ref[...] + square
 
-    for quad in range(quads - 1):
-        gather_home(quad)
-    with scope("gather0"):
-        gather(0)
+    gather_home(0)
     with scope("finish3"):
         finish(3)
-    for quad in range(1, quads):
+    for quad in range(quads):
         with scope("gather%d" % quad):
             gather(quad)
 
     def ready(chunk):
         at = pl.ds(pl.multiple_of(chunk * rows, rows), rows)
+        gains = gain_ref[...].astype(F32)
         gated, square = gate(quads - 1, at, pl.ds((quads - 1) * WIDE, WIDE))
         total = jnp.sum(ss_ref[at, :] + square, axis=1, keepdims=True)
         inv = lax.rsqrt(total * (1.0 / (quads * WIDE)) + 1e-05)
         for quad in range(quads):
-            gain = jnp.concatenate([gain_ref[2 * quad + i : 2 * quad + i + 1, :] for i in range(2)], axis=1)
+            gain = jnp.concatenate(
+                [gains[2 * quad + i : 2 * quad + i + 1, :] for i in range(2)], axis=1
+            )
             value = gated if quad == quads - 1 else ypart[quad, at, :]
             normed_ref[at, quad * WIDE : (quad + 1) * WIDE] = (
-                value * inv * gain.astype(F32)
+                value * inv * gain
             ).astype(BF16)
 
     def ring(step, way, sub):

time: 107 us -> 107 us (level)
  no operation moved by 1% of the time
where the time goes in v6:
time: 107 us
  Pallas kernels  106 us (99%)
    pallas_call x1, Pallas kernels, per_device(): pl.pallas_call(layer_kernel, out_shape=pltpu.VMEM((rows, wide), BF16), in...  106 us

profile of v6, /device:TPU:24, one launch (start us, length us, event | category | flops | bytes accessed | tf_op | source)
XLA Modules:
  0.0 106.5 jit_solution(17914660952847255819)
XLA Ops:
  0.0 105.6 %shard_map.127 = bf16[96,4096]{1,0:T(8,128)(2,1)S(1)} custom-call(bf16[768,1024]{1,0:T(8,128)(2,1)} %x_hbm.1, bf16[768,1024]{1,0:T(8,128)(2,1)} %z_hbm.1, bf16[768,256]{1,0:T(8,128)(2,1)} %bc_hbm.1, bf16[16,768]{1,0:T(8,128)(2,1)} %bitcast.3, s32[6,128]{1,0:T(8,128)} %bitcast.4, s32[16]{0:T(128)} %lengths_hbm.1, bf16[4,1024]{1,0:T(4,128)(2,1)} %convx_hbm.1, ...), custom_call_target="tpu_custom_call" | custom-call | tf_op jit(solution)/shard_map/pallas_call | solution.py:847
  105.6 0.9 copy.15

commit v7 on v6

--- a/solution.py
+++ b/solution.py
@@ -687,15 +687,6 @@
         return jnp.where(way == 0, back, lax.rem(mz + 1 + step, nhead))
 
     def one(step, _):
-        def ready_way(way, _):
-            @pl.when((step < nhead // 2) & ((step < nhead // 2 - 1) | (way == 0)))
-            def _():
-                ready(chunk_of(step, way))
-
-            return 0
-
-        lax.fori_loop(0, 2, ready_way, 0)
-
         @pl.when(step == nhead // 2)
         def _():
             ready(mz)
@@ -703,6 +694,12 @@
         for sub in range(SUBS):
             for way in range(2):
                 chunk = chunk_of(step, way)
+                if sub == 0:
+
+                    @pl.when((step < nhead // 2) & ((step < nhead // 2 - 1) | (way == 0)))
+                    def _():
+                        ready(chunk)
+
                 at = (way * SUBS + sub) * width
                 part = mm(
                     normed_ref[pl.ds(pl.multiple_of(chunk * rows, rows), rows), :],

time: 107 us -> 106 us (level)
  no operation moved by 1% of the time
where the time goes in v7:
time: 106 us
  Pallas kernels  105 us (99%)
    pallas_call x1, Pallas kernels, per_device(): pl.pallas_call(layer_kernel, out_shape=pltpu.VMEM((rows, wide), BF16), in...  105 us

profile of v7, /device:TPU:24, one launch (start us, length us, event | category | flops | bytes accessed | tf_op | source)
XLA Modules:
  0.0 106.2 jit_solution(15231625374975311855)
XLA Ops:
  0.0 105.4 %shard_map.127 = bf16[96,4096]{1,0:T(8,128)(2,1)S(1)} custom-call(bf16[768,1024]{1,0:T(8,128)(2,1)} %x_hbm.1, bf16[768,1024]{1,0:T(8,128)(2,1)} %z_hbm.1, bf16[768,256]{1,0:T(8,128)(2,1)} %bc_hbm.1, bf16[16,768]{1,0:T(8,128)(2,1)} %bitcast.3, s32[6,128]{1,0:T(8,128)} %bitcast.4, s32[16]{0:T(128)} %lengths_hbm.1, bf16[4,1024]{1,0:T(4,128)(2,1)} %convx_hbm.1, ...), custom_call_target="tpu_custom_call" | custom-call | tf_op jit(solution)/shard_map/pallas_call | solution.py:844
  105.4 0.9 copy.15
